TPU v7x, 512 devices: a whole 4x8x8 slice. The times are simulated.
512 devices in a mesh: rows: 64 (over y_lo, z, x), protos: 8 (over y_hi, core).
Axes of the slice: x: 4, y: 8 (y_hi: 4, y_lo: 2; y = y_hi * 2 + y_lo), z: 8, core: 2. Of those that a mesh axis runs over, the one named last changes fastest.
Arguments:
- embeddings: bfloat16 [65536, 1024], P('rows'), may hold values from -6 to 6
- prototypes: bfloat16 [8192, 1024], P('protos'), may hold values from -6 to 6
Outputs:
- codes: bfloat16 [65536, 8192], P('rows', 'protos')
- centers: bfloat16 [8192, 1024], P('protos')
All inputs are finite; a program needn't handle non-finite values.
Results may differ from a plain program's by a relative error of at most 0.004.
Values may be sent and summed in bfloat16 or wider, within the bound.
No kernel may reach another device: no remote copies, remote signals or barrier semaphores. Data moves between devices by JAX's collectives and lax.ppermute only.
A program may use at most 64 MiB of HBM per device.

v0:
```python
import jax
import jax.numpy as jnp
from jax import lax
from jax.sharding import PartitionSpec as P

ITERS = 3


def unit_norm(values):
    wide = values.astype(jnp.float32)
    total = jnp.sum(wide * wide, axis=1, keepdims=True)
    return (wide / jnp.sqrt(total + 1e-06)).astype(jnp.bfloat16)


def body(embeddings, prototypes):
    row_count = embeddings.shape[0] * lax.axis_size("rows")
    proto_count = prototypes.shape[0] * lax.axis_size("protos")
    unit_rows = unit_norm(embeddings)
    unit_protos = unit_norm(prototypes)
    kernel = jnp.exp(jnp.dot(unit_rows, unit_protos.T, preferred_element_type=jnp.float32) / 0.05)
    row_scale = jnp.ones((embeddings.shape[0],), jnp.float32)
    for step in range(ITERS):
        col_part = jnp.sum(kernel * row_scale[:, None], axis=0)
        col_scale = 1.0 / (proto_count * lax.psum(col_part, "rows"))
        row_part = jnp.sum(kernel * col_scale[None, :], axis=1)
        row_scale = 1.0 / (row_count * lax.psum(row_part, "protos"))
    codes = (
        float(row_count) * float(proto_count) * row_scale[:, None] * kernel * col_scale[None, :]
    ).astype(jnp.bfloat16)
    feature_width = embeddings.shape[1]
    term = lax.dot_general(
        codes, embeddings, (((0,), (0,)), ((), ())), preferred_element_type=jnp.float32
    )
    shares = lax.psum_scatter(term, "rows", scatter_dimension=1, tiled=True)
    squares = lax.psum(jnp.sum(shares * shares, axis=1), "rows")
    scaled = (shares / jnp.sqrt(squares[:, None] / feature_width + 1e-06)).astype(jnp.bfloat16)
    centers = lax.all_gather(scaled, "rows", axis=1, tiled=True)
    return (codes, centers)


def solution(mesh):
    return jax.shard_map(
        body,
        mesh=mesh,
        in_specs=(P("rows", None), P("protos", None)),
        out_specs=(P("rows", "protos"), P("protos", None)),
        check_vma=False,
    )
```

profile of v0, /device:TPU:56, one launch (start us, length us, event | category | flops | bytes accessed | tf_op | source)
XLA Modules:
  0.0 1332.0 jit_solution(213423113207824354)
XLA Ops:
  7.2 0.0 copy-start
  7.2 0.0 reduce-scatter.2.cloned.1.call-start
  7.2 0.0 copy-start.1
  7.2 2.2 fusion.2
  9.5 2.1 fusion
  11.5 0.0 copy-done
  11.6 4.4 fusion.8
  16.0 164.3 %psum.49 = f32[1024]{0:T(1024)S(1)} all-reduce(f32[1024]{0:T(1024)S(1)} %get-tuple-element.4), channel_id=1, replica_groups=mesh['rows'=64,'protos'=8] {'rows'}, use_global_device_ids=true, to_apply=%region_3.0 | all-reduce | flops 1024 | bytes 8192 | tf_op jit(solution)/shard_map/psum | solution.py:24
  180.3 2.5 multiply_reduce_fusion.4
  182.9 12.0 psum.50
  194.9 2.5 multiply_reduce_fusion.3
  197.4 152.4 %psum.51 = f32[1024]{0:T(1024)S(1)} all-reduce(f32[1024]{0:T(1024)S(1)} %multiply_reduce_fusion.3), channel_id=1, replica_groups=mesh['rows'=64,'protos'=8] {'rows'}, use_global_device_ids=true, to_apply=%region_7.0 | all-reduce | flops 1024 | bytes 8192 | tf_op jit(solution)/shard_map/psum | solution.py:24
  349.8 2.5 multiply_reduce_fusion.2
  352.3 14.2 %psum.52 = f32[1024]{0:T(1024)S(1)} all-reduce(f32[1024]{0:T(1024)S(1)} %multiply_reduce_fusion.2), channel_id=1, replica_groups=mesh['rows'=64,'protos'=8] {'protos'}, use_global_device_ids=true, to_apply=%region_9.0 | all-reduce | flops 1024 | bytes 8192 | tf_op jit(solution)/shard_map/psum | solution.py:26
  366.6 2.5 multiply_reduce_fusion.1
  369.1 154.4 %psum.53 = f32[1024]{0:T(1024)S(1)} all-reduce(f32[1024]{0:T(1024)S(1)} %multiply_reduce_fusion.1), channel_id=1, replica_groups=mesh['rows'=64,'protos'=8] {'rows'}, use_global_device_ids=true, to_apply=%region_11.0 | all-reduce | flops 1024 | bytes 8192 | tf_op jit(solution)/shard_map/psum | solution.py:24
  523.5 2.5 multiply_reduce_fusion
  526.0 0.0 copy-start.2
  526.0 14.4 %psum.54 = f32[1024]{0:T(1024)S(1)} all-reduce(f32[1024]{0:T(1024)S(1)} %multiply_reduce_fusion), channel_id=1, replica_groups=mesh['rows'=64,'protos'=8] {'protos'}, use_global_device_ids=true, to_apply=%region_13.0 | all-reduce | flops 1024 | bytes 8192 | tf_op jit(solution)/shard_map/psum | solution.py:26
  540.4 2.6 multiply_convert_fusion
  543.0 0.0 copy-start.3
  543.0 1.3 copy-done.3
  544.4 4.3 fusion.9
  548.7 0.0 reduce-scatter.2.cloned.1.call-update
  548.7 0.0 all-gather.2.cloned.1.call-start
  548.7 320.7 %reduce-scatter.2.cloned.1.call-done = f32[1024,16]{0,1:T(8,128)} async-done(((f32[1024,1024]{0,1:T(8,128)}), f32[1024,16]{0,1:T(8,128)}) %reduce-scatter.2.cloned.1.call-update) | async-done | bytes 65552 | tf_op jit(solution)/shard_map/reduce_scatter | solution.py:34
  869.5 0.9 multiply_reduce_fusion.5
  870.3 153.2 %psum.55 = f32[1024]{0:T(1024)S(1)} all-reduce(f32[1024]{0:T(1024)S(1)} %multiply_reduce_fusion.5), channel_id=1, replica_groups=mesh['rows'=64,'protos'=8] {'rows'}, use_global_device_ids=true, to_apply=%region_16.0 | all-reduce | flops 1024 | bytes 8192 | tf_op jit(solution)/shard_map/psum | solution.py:35
  1023.5 1.5 divide_convert_fusion
  1025.0 0.0 all-gather.2.cloned.1.call-update
  1025.0 296.2 %all-gather.2.cloned.1.call-done = bf16[1024,1024]{0,1:T(8,128)(2,1)} async-done(((bf16[1024,16]{0,1:T(8,128)(2,1)}), bf16[1024,1024]{0,1:T(8,128)(2,1)}) %all-gather.2.cloned.1.call-update) | async-done | bytes 2097168 | tf_op jit(solution)/shard_map/all_gather | solution.py:37
  1321.2 3.9 copy.4
  (10 shorter events, 0.1 us)
Async XLA Ops:
  7.2 4.4 copy-start
  7.2 862.3 %reduce-scatter.2.cloned.1.call-start = ((), (), s32[]{:S(2)}) async-start(), calls=%async_computation.1 | async-start | bytes 4259840 | tf_op jit(solution)/shard_map/reduce_scatter | solution.py:34
  7.2 4.3 copy-start.1
  526.0 18.3 %copy-start.2 = (bf16[1024,1024]{1,0:T(8,128)(2,1)S(1)}, bf16[1024,1024]{1,0:T(8,128)(2,1)}, u32[]{:S(2)}) copy-start(bf16[1024,1024]{1,0:T(8,128)(2,1)} %param.2) | copy-start | bytes 6291460
  543.0 1.3 copy-start.3
  548.7 772.5 %all-gather.2.cloned.1.call-start = ((), (), s32[]{:S(2)}) async-start(), calls=%async_computation.2 | async-start | bytes 2129920 | tf_op jit(solution)/shard_map/all_gather | solution.py:37
Sparse Core Ops, SparseCore 0:
  548.8 320.6 reduce-scatter.1
  1025.2 296.0 all-gather.1
where the time goes:
time: 1330 us
  blocking collectives  665 us (50%)
  waiting for transfers between devices  617 us (46%)
  other arithmetic  22 us (2%)
  between operations  14.1 us (1%)
    psum x3, blocking collectives, body(): col_scale = 1.0 / (proto_count * lax.psum(col_part, 'rows'))  471 us
    reduce_scatter x1, waiting for transfers between devices, body(): shares = lax.psum_scatter(term, 'rows', scatter_dimension=1, tiled=True)  321 us
    all_gather x1, waiting for transfers between devices, body(): centers = lax.all_gather(scaled, 'rows', axis=1, tiled=True)  296 us
    psum x1, blocking collectives, body(): squares = lax.psum(jnp.sum(shares * shares, axis=1), 'rows')  153 us
    psum x3, blocking collectives, body(): row_scale = 1.0 / (row_count * lax.psum(row_part, 'protos'))  40.6 us
  transfers between devices with their start and end apart: 2, of which 2 were waited for; matrix products, arithmetic and copies ran while one was open for 0% of the time, Pallas kernels for 0%

commit v1 on v0

v1 whole, which is shorter than its diff:
```python
import jax
import jax.numpy as jnp
from jax import lax
from jax.sharding import Mesh, PartitionSpec as P

ITERS = 3
ROWS = ("ylo", "zhi", "zlo", "x")
PROTOS = ("yhi", "core")
NEAR = ("ylo", "zlo", "x")
FAR = ("zhi",)
SIZES = {"ylo": 2, "zhi": 4, "zlo": 2, "x": 4, "yhi": 4, "core": 2}


def count(axes):
    total = 1
    for axis in axes:
        total *= SIZES[axis]
    return total


def exchange(blocks, axes):
    return lax.all_to_all(blocks, axes, 0, 0, tiled=True)


def everyone(block, axes):
    return exchange(jnp.broadcast_to(block[None], (count(axes), *block.shape)), axes)


def sum_small(vector, axes):
    return jnp.sum(everyone(vector.reshape(-1, 128), axes), axis=0).reshape(vector.shape)


def scatter_sum(blocks, axes):
    count_ = count(axes)
    split = blocks.reshape(count_, blocks.shape[0] // count_, blocks.shape[1])
    return jnp.sum(exchange(split.astype(jnp.bfloat16), axes).astype(jnp.float32), axis=0)


def gather(block, axes):
    return everyone(block, axes).reshape(-1, block.shape[-1])


def unit_norm(values):
    wide = values.astype(jnp.float32)
    total = jnp.sum(wide * wide, axis=1, keepdims=True)
    return (wide / jnp.sqrt(total + 1e-06)).astype(jnp.bfloat16)


def body(embeddings, prototypes):
    row_count = embeddings.shape[0] * count(ROWS)
    proto_count = prototypes.shape[0] * count(PROTOS)
    unit_rows = unit_norm(embeddings)
    unit_protos = unit_norm(prototypes)
    kernel = jnp.exp(jnp.dot(unit_rows, unit_protos.T, preferred_element_type=jnp.float32) / 0.05)
    row_scale = jnp.ones((embeddings.shape[0],), jnp.float32)
    for step in range(ITERS):
        col_part = jnp.sum(kernel * row_scale[:, None], axis=0)
        col_scale = 1.0 / (proto_count * sum_small(col_part, ROWS))
        row_part = jnp.sum(kernel * col_scale[None, :], axis=1)
        row_scale = 1.0 / (row_count * sum_small(row_part, PROTOS))
    codes = (
        float(row_count) * float(proto_count) * row_scale[:, None] * kernel * col_scale[None, :]
    ).astype(jnp.bfloat16)
    feature_width = embeddings.shape[1]
    term = lax.dot_general(
        codes, embeddings, (((0,), (0,)), ((), ())), preferred_element_type=jnp.float32
    )
    sums = scatter_sum(scatter_sum(term, NEAR), FAR)
    squares = jnp.sum(sums * sums, axis=1, keepdims=True)
    scaled = (sums / jnp.sqrt(squares / feature_width + 1e-06)).astype(jnp.bfloat16)
    centers = gather(gather(scaled, FAR), NEAR)
    return (codes, centers)


def solution(mesh):
    fine = Mesh(mesh.devices.reshape(tuple(SIZES.values())), tuple(SIZES))
    return jax.shard_map(
        body,
        mesh=fine,
        in_specs=(P(ROWS, None), P(PROTOS, None)),
        out_specs=(P(ROWS, PROTOS), P(PROTOS, None)),
        check_vma=False,
    )
```

time: 1330 us -> 208 us (0.16)
  waiting for transfers between devices: 617 us -> 0 us
  blocking collectives: 665 us -> 175 us
    psum x7 -> x0, blocking collectives: 665 us -> none  [the longest x3 471 us: body(): col_scale = 1.0 / (proto_count * lax.psum(col_part, 'rows'))]
    reduce_scatter x1 -> x0, waiting for transfers between devices: 321 us -> none  [body(): shares = lax.psum_scatter(term, 'rows', scatter_dimension=1, tiled=True)]
    all_gather x1 -> x0, waiting for transfers between devices: 296 us -> none  [body(): centers = lax.all_gather(scaled, 'rows', axis=1, tiled=True)]
    all_to_all x0 -> x10, blocking collectives: none -> 175 us  [exchange(): return lax.all_to_all(blocks, axes, 0, 0, tiled=True)]
  transfers between devices with their start and end apart: 2 -> 0, of which waited for: 2 -> 0; matrix products, arithmetic and copies ran while one was open for 0% -> 0% of each run, Pallas kernels for 0% -> 0%
where the time goes in v1:
time: 208 us; the launch traced here: 205 us
  blocking collectives  175 us (84%)
  other arithmetic  20.5 us (10%)
  matrix products  6.8 us (3%)
    all_to_all x10, blocking collectives, exchange(): return lax.all_to_all(blocks, axes, 0, 0, tiled=True)  175 us
    reduce_sum x3, other arithmetic, body(): row_part = jnp.sum(kernel * col_scale[None, :], axis=1)  7.61 us
    reduce_sum x2, other arithmetic, body(): col_part = jnp.sum(kernel * row_scale[:, None], axis=0)  5.07 us
    dot_general x1, matrix products, body(): jnp.dot(unit_rows, unit_protos.T, preferred_element_type=jnp.float32) / 0.05  4.41 us
    reduce_sum x2, other arithmetic, unit_norm(): total = jnp.sum(wide * wide, axis=1, keepdims=True)  4.29 us

profile of v1, /device:TPU:56, one launch (start us, length us, event | category | flops | bytes accessed | tf_op | source)
XLA Modules:
  0.0 204.6 jit_solution(109551037481808111)
XLA Ops:
  0.6 0.0 copy-start
  0.6 0.0 copy-start.1
  0.7 2.2 %fusion.2 = f32[1024]{0:T(1024)S(1)} fusion(bf16[1024,1024]{1,0:T(8,128)(2,1)} %param.3), kind=kLoop, calls=%fused_computation.6 | loop fusion | flops 3144704 | bytes 2101248 | tf_op jit(solution)/shard_map/reduce_sum | solution.py:45
  2.9 2.1 %fusion = f32[1024]{0:T(1024)S(1)} fusion(bf16[1024,1024]{1,0:T(8,128)(2,1)} %param.2), kind=kLoop, calls=%fused_computation.4 | loop fusion | flops 3144704 | bytes 2101248 | tf_op jit(solution)/shard_map/reduce_sum | solution.py:45
  5.0 0.0 copy-done
  5.0 4.4 %fusion.8 = (f32[1024]{0:T(1024)S(1)}, f32[1024,1024]{1,0:T(8,128)}) fusion(bf16[1024,1024]{1,0:T(8,128)(2,1)S(1)} %copy-done, f32[1024]{0:T(1024)S(1)} %get-tuple-element.4, bf16[1024,1024]{1,0:T(8,128)(2,1)S(1)} %copy-done.1, f32[1024]{0:T(1024)S(1)} %get-tuple-element.5), kind=kOutput, calls=%fused_computation.30 | convolution fusion | flops 2155871232 | bytes 8400896 | tf_op jit(solution)/shard_map/dot_general | solution.py:54
  9.4 26.0 %all_to_all.50 = f32[64,8,128]{2,1,0:T(8,128)S(1)} all-to-all(f32[64,8,128]{2,1,0:T(8,128)S(1)} %broadcast_in_dim.31), channel_id=1, replica_groups=mesh['ylo'=2,'zhi'=4,'zlo'=2,'x'=4,'yhi'=4,'core'=2] {'ylo','zhi','zlo',..., dimensions={0} | all-to-all | bytes 524288 | tf_op jit(solution)/shard_map/all_to_all | solution.py:22
  35.4 0.1 reduce_sum.159
  35.4 2.5 %multiply_reduce_fusion.4 = f32[1024]{0:T(1024)S(1)} fusion(f32[1024,1024]{1,0:T(8,128)} %get-tuple-element.3, f32[1024]{0:T(1024)S(1)} %divide_bitcast_fusion.4), kind=kLoop, calls=%fused_computation.13 | loop fusion | flops 2096128 | bytes 4202496 | tf_op jit(solution)/shard_map/reduce_sum | solution.py:59
  38.0 11.1 %all_to_all.51 = f32[8,8,128]{2,1,0:T(8,128)S(1)} all-to-all(f32[8,8,128]{2,1,0:T(8,128)S(1)} %broadcast_in_dim.33), channel_id=1, replica_groups=mesh['ylo'=2,'zhi'=4,'zlo'=2,'x'=4,'yhi'=4,'core'=2] {'yhi','core'}, dimensions={0} | all-to-all | bytes 65536 | tf_op jit(solution)/shard_map/all_to_all | solution.py:22
  49.1 2.5 %multiply_reduce_fusion.3 = f32[1024]{0:T(1024)S(1)} fusion(f32[1024,1024]{1,0:T(8,128)} %get-tuple-element.3, f32[1024]{0:T(1024)S(1)} %divide_bitcast_fusion.3), kind=kLoop, calls=%fused_computation.12 | loop fusion | flops 2096128 | bytes 4202496 | tf_op jit(solution)/shard_map/reduce_sum | solution.py:57
  51.6 17.9 %all_to_all.52 = f32[64,8,128]{2,1,0:T(8,128)S(1)} all-to-all(f32[64,8,128]{2,1,0:T(8,128)S(1)} %broadcast_in_dim.70), channel_id=1, replica_groups=mesh['ylo'=2,'zhi'=4,'zlo'=2,'x'=4,'yhi'=4,'core'=2] {'ylo','zhi','zlo',..., dimensions={0} | all-to-all | bytes 524288 | tf_op jit(solution)/shard_map/all_to_all | solution.py:22
  69.5 0.1 reduce_sum.163
  69.6 2.5 %multiply_reduce_fusion.2 = f32[1024]{0:T(1024)S(1)} fusion(f32[1024,1024]{1,0:T(8,128)} %get-tuple-element.3, f32[1024]{0:T(1024)S(1)} %divide_bitcast_fusion.2), kind=kLoop, calls=%fused_computation.11 | loop fusion | flops 2096128 | bytes 4202496 | tf_op jit(solution)/shard_map/reduce_sum | solution.py:59
  72.2 10.0 %all_to_all.53 = f32[8,8,128]{2,1,0:T(8,128)S(1)} all-to-all(f32[8,8,128]{2,1,0:T(8,128)S(1)} %broadcast_in_dim.72), channel_id=1, replica_groups=mesh['ylo'=2,'zhi'=4,'zlo'=2,'x'=4,'yhi'=4,'core'=2] {'yhi','core'}, dimensions={0} | all-to-all | bytes 65536 | tf_op jit(solution)/shard_map/all_to_all | solution.py:22
  82.2 2.5 %multiply_reduce_fusion.1 = f32[1024]{0:T(1024)S(1)} fusion(f32[1024,1024]{1,0:T(8,128)} %get-tuple-element.3, f32[1024]{0:T(1024)S(1)} %divide_bitcast_fusion.1), kind=kLoop, calls=%fused_computation.10 | loop fusion | flops 2096128 | bytes 4202496 | tf_op jit(solution)/shard_map/reduce_sum | solution.py:57
  84.7 17.9 %all_to_all.54 = f32[64,8,128]{2,1,0:T(8,128)S(1)} all-to-all(f32[64,8,128]{2,1,0:T(8,128)S(1)} %broadcast_in_dim.74), channel_id=1, replica_groups=mesh['ylo'=2,'zhi'=4,'zlo'=2,'x'=4,'yhi'=4,'core'=2] {'ylo','zhi','zlo',..., dimensions={0} | all-to-all | bytes 524288 | tf_op jit(solution)/shard_map/all_to_all | solution.py:22
  102.7 0.1 reduce_sum.167
  102.8 2.5 %multiply_reduce_fusion = f32[1024]{0:T(1024)S(1)} fusion(f32[1024,1024]{1,0:T(8,128)} %get-tuple-element.3, f32[1024]{0:T(1024)S(1)} %divide_bitcast_fusion), kind=kLoop, calls=%fused_computation.9 | loop fusion | flops 2096128 | bytes 4202496 | tf_op jit(solution)/shard_map/reduce_sum | solution.py:59
  105.3 10.0 %all_to_all.55 = f32[8,8,128]{2,1,0:T(8,128)S(1)} all-to-all(f32[8,8,128]{2,1,0:T(8,128)S(1)} %broadcast_in_dim.76), channel_id=1, replica_groups=mesh['ylo'=2,'zhi'=4,'zlo'=2,'x'=4,'yhi'=4,'core'=2] {'yhi','core'}, dimensions={0} | all-to-all | bytes 65536 | tf_op jit(solution)/shard_map/all_to_all | solution.py:22
  115.3 2.6 %multiply_convert_fusion = bf16[1024,1024]{1,0:T(8,128)(2,1)S(1)} fusion(f32[1024,1024]{1,0:T(8,128)} %get-tuple-element.3, f32[1024]{0:T(1024)S(1)} %multiply_bitcast_fusion, f32[1024]{0:T(1024)S(1)} %divide_bitcast_fusion), kind=kLoop, calls=%fused_computation.8 | loop fusion | flops 3145728 | bytes 6299648 | tf_op jit(solution)/shard_map/convert_element_type | solution.py:63
  117.9 0.0 copy-start.2
  117.9 2.4 %convolution_convert_fusion = bf16[1024,1024]{1,0:T(8,128)(2,1)S(1)} fusion(bf16[1024,1024]{1,0:T(8,128)(2,1)S(1)} %multiply_convert_fusion, bf16[1024,1024]{1,0:T(8,128)(2,1)S(1)} %copy-done.1), kind=kOutput, calls=%fused_computation.17 | convolution fusion | flops 2148532224 | bytes 6291456 | tf_op jit(solution)/shard_map/dot_general | solution.py:65
  120.3 32.3 %all_to_all.56 = bf16[16,64,1024]{2,1,0:T(8,128)(2,1)S(1)} all-to-all(bf16[16,64,1024]{2,1,0:T(8,128)(2,1)S(1)} %bitcast.25), channel_id=1, replica_groups=mesh['ylo'=2,'zhi'=4,'zlo'=2,'x'=4,'yhi'=4,'core'=2] {'ylo','zlo','x'}, dimensions={0} | all-to-all | bytes 4194304 | tf_op jit(solution)/shard_map/all_to_all | solution.py:22
  152.6 0.4 reduce_sum.170
  153.0 11.9 %all_to_all.57 = bf16[4,16,1024]{2,1,0:T(8,128)(2,1)S(1)} all-to-all(bf16[4,16,1024]{2,1,0:T(8,128)(2,1)S(1)} %bitcast.26), channel_id=1, replica_groups=mesh['ylo'=2,'zhi'=4,'zlo'=2,'x'=4,'yhi'=4,'core'=2] {'zhi'}, dimensions={0} | all-to-all | bytes 262144 | tf_op jit(solution)/shard_map/all_to_all | solution.py:22
  165.0 0.1 multiply_reduce_fusion.5
  165.1 0.1 divide_convert_fusion
  165.2 10.8 %all_to_all.58 = bf16[4,16,1024]{2,1,0:T(8,128)(2,1)S(1)} all-to-all(bf16[4,16,1024]{2,1,0:T(8,128)(2,1)S(1)} %broadcast_in_dim.77), channel_id=1, replica_groups=mesh['ylo'=2,'zhi'=4,'zlo'=2,'x'=4,'yhi'=4,'core'=2] {'zhi'}, dimensions={0} | all-to-all | bytes 262144 | tf_op jit(solution)/shard_map/all_to_all | solution.py:22
  176.0 0.2 broadcast_in_dim.79
  176.2 27.0 %all_to_all.59 = bf16[16,64,1024]{2,1,0:T(8,128)(2,1)S(1)} all-to-all(bf16[16,64,1024]{2,1,0:T(8,128)(2,1)S(1)} %broadcast_in_dim.79), channel_id=1, replica_groups=mesh['ylo'=2,'zhi'=4,'zlo'=2,'x'=4,'yhi'=4,'core'=2] {'ylo','zlo','x'}, dimensions={0} | all-to-all | bytes 4194304 | tf_op jit(solution)/shard_map/all_to_all | solution.py:22
  203.3 1.3 copy.5
  (21 shorter events, 0.2 us)
Async XLA Ops:
  0.6 4.3 %copy-start = (bf16[1024,1024]{1,0:T(8,128)(2,1)S(1)}, bf16[1024,1024]{1,0:T(8,128)(2,1)}, u32[]{:S(2)}) copy-start(bf16[1024,1024]{1,0:T(8,128)(2,1)} %param.3) | copy-start | bytes 6291460
  0.6 4.3 %copy-start.1 = (bf16[1024,1024]{1,0:T(8,128)(2,1)S(1)}, bf16[1024,1024]{1,0:T(8,128)(2,1)}, u32[]{:S(2)}) copy-start(bf16[1024,1024]{1,0:T(8,128)(2,1)} %param.2) | copy-start | bytes 6291460
  117.9 2.4 %copy-start.2 = (bf16[1024,1024]{1,0:T(8,128)(2,1)}, bf16[1024,1024]{1,0:T(8,128)(2,1)S(1)}, u32[]{:S(2)}) copy-start(bf16[1024,1024]{1,0:T(8,128)(2,1)S(1)} %multiply_convert_fusion) | copy-start | bytes 6291460

commit v2 on v1

v2 whole, which is shorter than its diff:
```python
import functools

import jax
import jax.numpy as jnp
from jax import lax
from jax.experimental import pallas as pl
from jax.experimental.pallas import tpu as pltpu
from jax.sharding import Mesh, PartitionSpec as P

ITERS = 3
LANES = 128
ROWS = ("ylo", "zhi", "zlo", "x")
PROTOS = ("yhi", "core")
NEAR = ("ylo", "zlo", "x")
FAR = ("zhi",)
SIZES = {"ylo": 2, "zhi": 4, "zlo": 2, "x": 4, "yhi": 4, "core": 2}


def count(axes):
    total = 1
    for axis in axes:
        total *= SIZES[axis]
    return total


def exchange(blocks, axes):
    return lax.all_to_all(blocks, axes, 0, 0, tiled=True)


def everyone(block, axes):
    return exchange(jnp.broadcast_to(block[None], (count(axes), *block.shape)), axes)


def on_chip(body, out_shape, operands, flops, moved):
    spec = pl.BlockSpec(memory_space=pltpu.VMEM)
    return pl.pallas_call(
        body,
        out_shape=out_shape,
        in_specs=[spec] * len(operands),
        out_specs=jax.tree.map(lambda _: spec, out_shape),
        compiler_params=pltpu.CompilerParams(vmem_limit_bytes=40 * 1024 * 1024),
        cost_estimate=pl.CostEstimate(flops=flops, bytes_accessed=moved, transcendentals=0),
    )(*operands)


def blocks_of(size):
    return [slice(start, start + LANES) for start in range(0, size, LANES)]


def down_rows(line):
    return jnp.broadcast_to(line, (LANES, LANES)).T


def row_body(scale, kernel_ref, parts_ref, col_ref, out_ref):
    col_scale = 1.0 / (scale * jnp.sum(parts_ref[...], axis=0))
    col_ref[...] = col_scale
    lines = []
    for rows in blocks_of(kernel_ref.shape[0]):
        total = None
        for k, lanes in enumerate(blocks_of(kernel_ref.shape[1])):
            tile = kernel_ref[rows, lanes] * col_scale[k : k + 1, :]
            total = tile if total is None else total + tile
        lines.append(jnp.sum(total.T, axis=0, keepdims=True))
    out_ref[...] = jnp.broadcast_to(jnp.concatenate(lines, axis=0)[None], out_ref.shape)


def col_body(scale, kernel_ref, parts_ref, out_ref):
    row_scale = 1.0 / (scale * jnp.sum(parts_ref[...], axis=0))
    totals = [None] * (kernel_ref.shape[1] // LANES)
    for r, rows in enumerate(blocks_of(kernel_ref.shape[0])):
        turned = down_rows(row_scale[r : r + 1, :])
        for k, lanes in enumerate(blocks_of(kernel_ref.shape[1])):
            tile = kernel_ref[rows, lanes] * turned
            part = jnp.sum(tile.reshape(LANES // 8, 8, LANES), axis=0)
            totals[k] = part if totals[k] is None else totals[k] + part
    lines = [jnp.sum(total, axis=0, keepdims=True) for total in totals]
    out_ref[...] = jnp.broadcast_to(jnp.concatenate(lines, axis=0)[None], out_ref.shape)


def codes_body(scale, mass, kernel_ref, parts_ref, col_ref, codes_ref):
    row_scale = mass / (scale * jnp.sum(parts_ref[...], axis=0))
    col_scale = col_ref[...]
    for r, rows in enumerate(blocks_of(kernel_ref.shape[0])):
        turned = down_rows(row_scale[r : r + 1, :])
        for k, lanes in enumerate(blocks_of(kernel_ref.shape[1])):
            tile = turned * kernel_ref[rows, lanes] * col_scale[k : k + 1, :]
            codes_ref[rows, lanes] = tile.astype(jnp.bfloat16)


def unit_norm(values):
    wide = values.astype(jnp.float32)
    total = jnp.sum(wide * wide, axis=1, keepdims=True)
    return (wide / jnp.sqrt(total + 1e-06)).astype(jnp.bfloat16)


def body(embeddings, prototypes):
    rows, protos = embeddings.shape[0], prototypes.shape[0]
    row_count = float(rows * count(ROWS))
    proto_count = float(protos * count(PROTOS))
    unit_rows = unit_norm(embeddings)
    unit_protos = unit_norm(prototypes)
    kernel = jnp.exp(jnp.dot(unit_rows, unit_protos.T, preferred_element_type=jnp.float32) / 0.05)
    line_rows = jax.ShapeDtypeStruct((rows // LANES, LANES), jnp.float32)
    line_protos = jax.ShapeDtypeStruct((protos // LANES, LANES), jnp.float32)
    copies_rows = jax.ShapeDtypeStruct((count(PROTOS), *line_rows.shape), jnp.float32)
    copies_protos = jax.ShapeDtypeStruct((count(ROWS), *line_protos.shape), jnp.float32)
    work = 2 * rows * protos
    col_parts = everyone(jnp.sum(kernel, axis=0).reshape(line_protos.shape), ROWS)
    for step in range(ITERS):
        col_scale, row_sums = on_chip(
            functools.partial(row_body, proto_count),
            (line_protos, copies_rows),
            (kernel, col_parts),
            work,
            2 * work,
        )
        row_parts = exchange(row_sums, PROTOS)
        if step < ITERS - 1:
            col_sums = on_chip(
                functools.partial(col_body, row_count),
                copies_protos,
                (kernel, row_parts),
                work,
                2 * work,
            )
            col_parts = exchange(col_sums, ROWS)
    codes = on_chip(
        functools.partial(codes_body, row_count, row_count * proto_count),
        jax.ShapeDtypeStruct(kernel.shape, jnp.bfloat16),
        (kernel, row_parts, col_scale),
        work,
        3 * work,
    )
    feature_width = embeddings.shape[1]
    term = lax.dot_general(
        codes, embeddings, (((0,), (0,)), ((), ())), preferred_element_type=jnp.float32
    ).astype(jnp.bfloat16)
    near = exchange(term.reshape(count(NEAR), -1, feature_width), NEAR)
    near = jnp.sum(near.astype(jnp.float32), axis=0).astype(jnp.bfloat16)
    sums = jnp.sum(everyone(near, FAR).astype(jnp.float32), axis=0)
    squares = jnp.sum(sums * sums, axis=1, keepdims=True)
    scaled = (sums / jnp.sqrt(squares / feature_width + 1e-06)).astype(jnp.bfloat16)
    return (codes, everyone(scaled, NEAR).reshape(prototypes.shape))


def solution(mesh):
    fine = Mesh(mesh.devices.reshape(tuple(SIZES.values())), tuple(SIZES))
    return jax.shard_map(
        body,
        mesh=fine,
        in_specs=(P(ROWS, None), P(PROTOS, None)),
        out_specs=(P(ROWS, PROTOS), P(PROTOS, None)),
        check_vma=False,
    )
```

time: 208 us -> 194 us (0.933)
  other arithmetic: 20.5 us -> 5 us
  Pallas kernels: 0 us -> 4.9 us
  blocking collectives: 175 us -> 172 us
    reduce_sum x13 -> x2, other arithmetic: 13.3 us -> 0.47 us  [the longest x1 0.4 us: body(): near = jnp.sum(near.astype(jnp.float32), axis=0).astype(jnp.bfloat16)]
    pallas_call x0 -> x6, Pallas kernels: none -> 4.9 us  [on_chip(): pl.pallas_call(body, out_shape=out_shape, in_specs=[spec] * len(operands)...]
    convert_element_type x1 -> x0, other arithmetic: 2.6 us -> none  [body(): codes = (float(row_count) * float(proto_count) * row_scale[:, None] * ker...]
    all_to_all x10 -> x9, blocking collectives: 175 us -> 172 us  [exchange(): return lax.all_to_all(blocks, axes, 0, 0, tiled=True)]
where the time goes in v2:
time: 194 us; the launch traced here: 191 us
  blocking collectives  172 us (89%)
  matrix products  6.47 us (3%)
  other arithmetic  5 us (3%)
  Pallas kernels  4.9 us (3%)
    all_to_all x9, blocking collectives, exchange(): return lax.all_to_all(blocks, axes, 0, 0, tiled=True)  172 us
    pallas_call x6, Pallas kernels, on_chip(): pl.pallas_call(body, out_shape=out_shape, in_specs=[spec] * len(operands)...  4.9 us
    reduce_sum x2, other arithmetic, unit_norm(): total = jnp.sum(wide * wide, axis=1, keepdims=True)  4.29 us
    dot_general x1, matrix products, body(): lax.dot_general(codes, embeddings, (((0,), (0,)), ((), ())), preferred_el...  3.97 us

profile of v2, /device:TPU:56, one launch (start us, length us, event | category | flops | bytes accessed | tf_op | source)
XLA Modules:
  0.0 191.0 jit_solution(12829890745721450082)
XLA Ops:
  0.6 0.0 copy-start
  0.6 0.0 copy-start.1
  0.7 2.2 %fusion.2 = f32[1024]{0:T(1024)S(1)} fusion(bf16[1024,1024]{1,0:T(8,128)(2,1)} %param.3), kind=kLoop, calls=%fused_computation.6 | loop fusion | flops 3144704 | bytes 2101248 | tf_op jit(solution)/shard_map/reduce_sum | solution.py:92
  2.9 2.1 %fusion = f32[1024]{0:T(1024)S(1)} fusion(bf16[1024,1024]{1,0:T(8,128)(2,1)} %param.2), kind=kLoop, calls=%fused_computation.4 | loop fusion | flops 3144704 | bytes 2101248 | tf_op jit(solution)/shard_map/reduce_sum | solution.py:92
  5.0 0.0 copy-done
  5.0 0.0 copy-done.1
  5.0 2.5 %fusion.8 = (f32[1024]{0:T(1024)S(1)}, f32[1024,1024]{1,0:T(8,128)S(1)}) fusion(bf16[1024,1024]{1,0:T(8,128)(2,1)S(1)} %copy-done, f32[1024]{0:T(1024)S(1)} %get-tuple-element.12, bf16[1024,1024]{1,0:T(8,128)(2,1)S(1)} %copy-done.1, f32[1024]{0:T(1024)S(1)} %get-tuple-element.13), kind=kOutput, calls=%fused_computation.18 | convolution fusion | flops 2155871232 | bytes 8400896 | tf_op jit(solution)/shard_map/dot_general | solution.py:102
  7.5 25.9 %all_to_all.45.parts_ref = f32[64,8,128]{2,1,0:T(8,128)S(1)} all-to-all(f32[64,8,128]{2,1,0:T(8,128)S(1)} %broadcast_in_dim.9), channel_id=1, replica_groups=mesh['ylo'=2,'zhi'=4,'zlo'=2,'x'=4,'yhi'=4,'core'=2] {'ylo','zhi','zlo',..., dimensions={0} | all-to-all | bytes 524288 | tf_op jit(solution)/shard_map/all_to_all | solution.py:27
  33.5 0.9 shard_map.41
  34.4 11.0 %all_to_all.46.parts_ref = f32[8,8,128]{2,1,0:T(8,128)S(1)} all-to-all(f32[8,8,128]{2,1,0:T(8,128)S(1)} %get-tuple-element.6), channel_id=1, replica_groups=mesh['ylo'=2,'zhi'=4,'zlo'=2,'x'=4,'yhi'=4,'core'=2] {'yhi','core'}, dimensions={0} | all-to-all | bytes 65536 | tf_op jit(solution)/shard_map/all_to_all | solution.py:27
  45.4 0.4 shard_map.42
  45.8 17.9 %all_to_all.47.parts_ref = f32[64,8,128]{2,1,0:T(8,128)S(1)} all-to-all(f32[64,8,128]{2,1,0:T(8,128)S(1)} %shard_map.42), channel_id=1, replica_groups=mesh['ylo'=2,'zhi'=4,'zlo'=2,'x'=4,'yhi'=4,'core'=2] {'ylo','zhi','zlo',..., dimensions={0} | all-to-all | bytes 524288 | tf_op jit(solution)/shard_map/all_to_all | solution.py:27
  63.7 0.9 shard_map.43
  64.7 10.0 %all_to_all.48.parts_ref = f32[8,8,128]{2,1,0:T(8,128)S(1)} all-to-all(f32[8,8,128]{2,1,0:T(8,128)S(1)} %get-tuple-element.7), channel_id=1, replica_groups=mesh['ylo'=2,'zhi'=4,'zlo'=2,'x'=4,'yhi'=4,'core'=2] {'yhi','core'}, dimensions={0} | all-to-all | bytes 65536 | tf_op jit(solution)/shard_map/all_to_all | solution.py:27
  74.6 0.4 shard_map.44
  75.0 17.9 %all_to_all.49.parts_ref = f32[64,8,128]{2,1,0:T(8,128)S(1)} all-to-all(f32[64,8,128]{2,1,0:T(8,128)S(1)} %shard_map.44), channel_id=1, replica_groups=mesh['ylo'=2,'zhi'=4,'zlo'=2,'x'=4,'yhi'=4,'core'=2] {'ylo','zhi','zlo',..., dimensions={0} | all-to-all | bytes 524288 | tf_op jit(solution)/shard_map/all_to_all | solution.py:27
  92.9 0.4 shard_map.45
  93.4 10.0 %all_to_all.50.parts_ref = f32[8,8,128]{2,1,0:T(8,128)S(1)} all-to-all(f32[8,8,128]{2,1,0:T(8,128)S(1)} %get-tuple-element.8), channel_id=1, replica_groups=mesh['ylo'=2,'zhi'=4,'zlo'=2,'x'=4,'yhi'=4,'core'=2] {'yhi','core'}, dimensions={0} | all-to-all | bytes 65536 | tf_op jit(solution)/shard_map/all_to_all | solution.py:27
  103.3 1.9 shard_map.46
  105.2 4.0 %convolution_convert_fusion = bf16[1024,1024]{1,0:T(8,128)(2,1)S(1)} fusion(bf16[1024,1024]{1,0:T(8,128)(2,1)} %shard_map.46, bf16[1024,1024]{1,0:T(8,128)(2,1)S(1)} %copy-done.1), kind=kOutput, calls=%fused_computation.11 | convolution fusion | flops 2148532224 | bytes 6291456 | tf_op jit(solution)/shard_map/dot_general | solution.py:135
  109.2 32.3 %all_to_all.51 = bf16[16,64,1024]{2,1,0:T(8,128)(2,1)S(1)} all-to-all(bf16[16,64,1024]{2,1,0:T(8,128)(2,1)S(1)} %bitcast.6), channel_id=1, replica_groups=mesh['ylo'=2,'zhi'=4,'zlo'=2,'x'=4,'yhi'=4,'core'=2] {'ylo','zlo','x'}, dimensions={0} | all-to-all | bytes 4194304 | tf_op jit(solution)/shard_map/all_to_all | solution.py:27
  141.5 0.4 reduce_sum.60
  141.9 0.1 broadcast_in_dim.10
  142.0 17.8 %all_to_all.52 = bf16[4,64,1024]{2,1,0:T(8,128)(2,1)S(1)} all-to-all(bf16[4,64,1024]{2,1,0:T(8,128)(2,1)S(1)} %broadcast_in_dim.10), channel_id=1, replica_groups=mesh['ylo'=2,'zhi'=4,'zlo'=2,'x'=4,'yhi'=4,'core'=2] {'zhi'}, dimensions={0} | all-to-all | bytes 1048576 | tf_op jit(solution)/shard_map/all_to_all | solution.py:27
  159.8 0.1 convert_reduce_fusion
  159.9 0.1 multiply_reduce_fusion
  160.0 0.1 divide_convert_fusion
  160.1 0.3 broadcast_in_dim.11
  160.4 29.3 %all_to_all.53 = bf16[16,64,1024]{2,1,0:T(8,128)(2,1)S(1)} all-to-all(bf16[16,64,1024]{2,1,0:T(8,128)(2,1)S(1)} %broadcast_in_dim.11), channel_id=1, replica_groups=mesh['ylo'=2,'zhi'=4,'zlo'=2,'x'=4,'yhi'=4,'core'=2] {'ylo','zlo','x'}, dimensions={0} | all-to-all | bytes 4194304 | tf_op jit(solution)/shard_map/all_to_all | solution.py:27
  189.7 1.3 copy.5
  (3 shorter events, 0.0 us)
Async XLA Ops:
  0.6 4.3 %copy-start = (bf16[1024,1024]{1,0:T(8,128)(2,1)S(1)}, bf16[1024,1024]{1,0:T(8,128)(2,1)}, u32[]{:S(2)}) copy-start(bf16[1024,1024]{1,0:T(8,128)(2,1)} %param.3) | copy-start | bytes 6291460
  0.6 4.3 %copy-start.1 = (bf16[1024,1024]{1,0:T(8,128)(2,1)S(1)}, bf16[1024,1024]{1,0:T(8,128)(2,1)}, u32[]{:S(2)}) copy-start(bf16[1024,1024]{1,0:T(8,128)(2,1)} %param.2) | copy-start | bytes 6291460

commit v3 on v2

v3 whole, which is shorter than its diff:
```python
import functools

import jax
import jax.numpy as jnp
from jax import lax
from jax.experimental import pallas as pl
from jax.experimental.pallas import tpu as pltpu
from jax.sharding import Mesh, PartitionSpec as P

ITERS = 3
LANES = 128
ROWS = ("ylo", "zhi", "zlo", "x")
PROTOS = ("yhi", "core")
NEAR = ("ylo", "zlo", "x")
FAR = ("zhi",)
SIZES = {"ylo": 2, "zhi": 4, "zlo": 2, "x": 4, "yhi": 4, "core": 2}


def count(axes):
    total = 1
    for axis in axes:
        total *= SIZES[axis]
    return total


def exchange(blocks, axes):
    return lax.all_to_all(blocks, axes, 0, 0, tiled=True)


def everyone(block, axes):
    return exchange(jnp.broadcast_to(block[None], (count(axes), *block.shape)), axes)


def on_chip(body, out_shape, operands, flops, moved):
    spec = pl.BlockSpec(memory_space=pltpu.VMEM)
    return pl.pallas_call(
        body,
        out_shape=out_shape,
        in_specs=[spec] * len(operands),
        out_specs=jax.tree.map(lambda _: spec, out_shape),
        compiler_params=pltpu.CompilerParams(vmem_limit_bytes=40 * 1024 * 1024),
        cost_estimate=pl.CostEstimate(flops=flops, bytes_accessed=moved, transcendentals=0),
    )(*operands)


def blocks_of(size):
    return [slice(start, start + LANES) for start in range(0, size, LANES)]


def down_rows(line):
    return jnp.broadcast_to(line, (LANES, LANES)).T


def load_body(halves, rows_in, protos_in, rows_ref, protos_ref, rows_inv, protos_inv, sems):
    steps = []
    for which, (source, target, inverse) in enumerate(
        ((rows_in, rows_ref, rows_inv), (protos_in, protos_ref, protos_inv))
    ):
        size = source.shape[0] // halves
        for half in range(halves):
            part = pl.ds(half * size, size)
            copy = pltpu.make_async_copy(
                source.at[part, :], target.at[part, :], sems.at[which * halves + half]
            )
            copy.start()
            lines = range(half * size // LANES, (half + 1) * size // LANES)
            steps.append((copy, target, inverse, lines))
    for copy, target, inverse, lines in steps:
        copy.wait()
        for line in lines:
            rows = slice(line * LANES, (line + 1) * LANES)
            total = None
            for lanes in blocks_of(target.shape[1]):
                tile = target[rows, lanes].astype(jnp.float32)
                total = tile * tile if total is None else total + tile * tile
            square = jnp.sum(total.T, axis=0, keepdims=True)
            inverse[line : line + 1, :] = 1.0 / jnp.sqrt(square + 1e-06)


def load(embeddings, prototypes):
    halves = 2
    vmem = pl.BlockSpec(memory_space=pltpu.VMEM)
    whole = pl.BlockSpec(memory_space=pl.ANY)
    arrays = (embeddings, prototypes)
    return pl.pallas_call(
        functools.partial(load_body, halves),
        out_shape=(
            *(jax.ShapeDtypeStruct(a.shape, a.dtype) for a in arrays),
            *(jax.ShapeDtypeStruct((a.shape[0] // LANES, LANES), jnp.float32) for a in arrays),
        ),
        in_specs=[whole, whole],
        out_specs=(vmem,) * 4,
        scratch_shapes=[pltpu.SemaphoreType.DMA((2 * halves,))],
        compiler_params=pltpu.CompilerParams(vmem_limit_bytes=40 * 1024 * 1024),
        cost_estimate=pl.CostEstimate(
            flops=4 * embeddings.size, bytes_accessed=8 * embeddings.size, transcendentals=0
        ),
    )(*arrays)


def send(lines, out_ref):
    block = jnp.concatenate(lines, axis=0).astype(out_ref.dtype)
    out_ref[...] = jnp.broadcast_to(block[None], out_ref.shape)


def row_body(scale, kernel_ref, parts_ref, out_ref):
    col_scale = 1.0 / (scale * jnp.sum(parts_ref[...].astype(jnp.float32), axis=0))
    lines = []
    for rows in blocks_of(kernel_ref.shape[0]):
        total = None
        for k, lanes in enumerate(blocks_of(kernel_ref.shape[1])):
            tile = kernel_ref[rows, lanes] * col_scale[k : k + 1, :]
            total = tile if total is None else total + tile
        lines.append(jnp.sum(total.T, axis=0, keepdims=True))
    send(lines, out_ref)


def col_body(scale, kernel_ref, parts_ref, out_ref):
    row_scale = 1.0 / (scale * jnp.sum(parts_ref[...], axis=0))
    totals = [None] * (kernel_ref.shape[1] // LANES)
    for r, rows in enumerate(blocks_of(kernel_ref.shape[0])):
        turned = down_rows(row_scale[r : r + 1, :])
        for k, lanes in enumerate(blocks_of(kernel_ref.shape[1])):
            tile = kernel_ref[rows, lanes] * turned
            part = jnp.sum(tile.reshape(LANES // 8, 8, LANES), axis=0)
            totals[k] = part if totals[k] is None else totals[k] + part
    lines = [jnp.sum(total, axis=0, keepdims=True) for total in totals]
    send(lines, out_ref)


def unit(values, inverse):
    return (values.astype(jnp.float32) * inverse.reshape(-1, 1)).astype(jnp.bfloat16)


def body(embeddings, prototypes):
    rows, protos = embeddings.shape[0], prototypes.shape[0]
    row_count = float(rows * count(ROWS))
    proto_count = float(protos * count(PROTOS))
    embeddings, prototypes, row_inverse, proto_inverse = load(embeddings, prototypes)
    dots = jnp.dot(
        unit(embeddings, row_inverse),
        unit(prototypes, proto_inverse).T,
        preferred_element_type=jnp.float32,
    )
    kernel = jnp.exp(dots / 0.05)
    line_rows = (rows // LANES, LANES)
    line_protos = (protos // LANES, LANES)
    work = 2 * rows * protos
    first = jnp.sum(kernel, axis=0).reshape(line_protos).astype(jnp.bfloat16)
    col_parts = everyone(first, ROWS)
    for step in range(ITERS):
        row_sums = on_chip(
            functools.partial(row_body, proto_count),
            jax.ShapeDtypeStruct((count(PROTOS), *line_rows), jnp.float32),
            (kernel, col_parts),
            work,
            2 * work,
        )
        row_parts = exchange(row_sums, PROTOS)
        if step < ITERS - 1:
            kind = jnp.float32 if step == ITERS - 2 else jnp.bfloat16
            col_sums = on_chip(
                functools.partial(col_body, row_count),
                jax.ShapeDtypeStruct((count(ROWS), *line_protos), kind),
                (kernel, row_parts),
                work,
                2 * work,
            )
            col_parts = exchange(col_sums, ROWS)
    col_scale = (1.0 / (proto_count * jnp.sum(col_parts, axis=0))).reshape(1, protos)
    row_scale = (1.0 / (row_count * jnp.sum(row_parts, axis=0))).reshape(rows, 1)
    codes = (row_count * proto_count * row_scale * kernel * col_scale).astype(jnp.bfloat16)
    feature_width = embeddings.shape[1]
    term = lax.dot_general(
        codes, embeddings, (((0,), (0,)), ((), ())), preferred_element_type=jnp.float32
    ).astype(jnp.bfloat16)
    near = exchange(term.reshape(count(NEAR), -1, feature_width), NEAR)
    near = jnp.sum(near.astype(jnp.float32), axis=0).astype(jnp.bfloat16)
    sums = jnp.sum(everyone(near, FAR).astype(jnp.float32), axis=0)
    squares = jnp.sum(sums * sums, axis=1, keepdims=True)
    scaled = (sums / jnp.sqrt(squares / feature_width + 1e-06)).astype(jnp.bfloat16)
    return (codes, everyone(scaled, NEAR).reshape(protos, feature_width))


def solution(mesh):
    fine = Mesh(mesh.devices.reshape(tuple(SIZES.values())), tuple(SIZES))
    return jax.shard_map(
        body,
        mesh=fine,
        in_specs=(P(ROWS, None), P(PROTOS, None)),
        out_specs=(P(ROWS, PROTOS), P(PROTOS, None)),
        check_vma=False,
    )
```

time: 194 us -> 189 us (0.974)
  blocking collectives: 172 us -> 157 us
  starting transfers between devices: 0 us -> 6.61 us
  waiting for transfers between devices: 0 us -> 4.18 us
  local copies, waits for them, and re-layouts: 1.65 us -> 4.82 us
    all_to_all x9 -> x8, blocking collectives: 172 us -> 157 us  [exchange(): return lax.all_to_all(blocks, axes, 0, 0, tiled=True)]
    all_to_all x0 -> x1, starting transfers between devices: none -> 6.61 us  [exchange(): return lax.all_to_all(blocks, axes, 0, 0, tiled=True)]
    reduce_sum x2, other arithmetic: 4.29 us -> 0.08 us  [the longest x1 0.07 us: body(): jnp.sum(col_parts, axis=0)]
    all_to_all x0 -> x1, waiting for transfers between devices: none -> 4.18 us  [exchange(): return lax.all_to_all(blocks, axes, 0, 0, tiled=True)]
    unnamed x5 -> x9, local copies, waits for them, and re-layouts: 1.33 us -> 4.5 us
    convert_element_type x0 -> x1, other arithmetic: none -> 2.6 us  [body(): (row_count * proto_count * row_scale * kernel * col_scale).astype(jnp.bfl...]
    pallas_call x6 -> x5, Pallas kernels: 4.9 us -> 2.61 us  [on_chip(): pl.pallas_call(body, out_shape=out_shape, in_specs=[spec] * len(operands)...]
  transfers between devices with their start and end apart: 0 -> 1, of which waited for: 0 -> 1; matrix products, arithmetic and copies ran while one was open for 0% -> 0% of each run, Pallas kernels for 0% -> 0%
where the time goes in v3:
time: 189 us; the launch traced here: 185 us
  blocking collectives  157 us (83%)
  starting transfers between devices  6.61 us (3%)
  matrix products  4.86 us (3%)
  local copies, waits for them, and re-layouts  4.82 us (3%)
  waiting for transfers between devices  4.18 us (2%)
  Pallas kernels  4.09 us (2%)
  other arithmetic  3.4 us (2%)
    all_to_all x8, blocking collectives, exchange(): return lax.all_to_all(blocks, axes, 0, 0, tiled=True)  157 us
    all_to_all x1, starting transfers between devices, exchange(): return lax.all_to_all(blocks, axes, 0, 0, tiled=True)  6.61 us
    unnamed x9, local copies, waits for them, and re-layouts  4.5 us
    all_to_all x1, waiting for transfers between devices, exchange(): return lax.all_to_all(blocks, axes, 0, 0, tiled=True)  4.18 us
  transfers between devices with their start and end apart: 1, of which 1 were waited for; matrix products, arithmetic and copies ran while one was open for 0% of the time, Pallas kernels for 0%

profile of v3, /device:TPU:56, one launch (start us, length us, event | category | flops | bytes accessed | tf_op | source)
XLA Modules:
  0.0 185.5 jit_solution(15430126251946288431)
XLA Ops:
  0.6 0.0 copy-start.1
  0.6 1.6 copy-done.1
  2.2 1.6 copy-done.2
  3.8 1.5 shard_map.41
  5.3 2.5 %fusion.2 = (bf16[1024]{0:T(1024)(128)(2,1)S(1)}, f32[1024,1024]{1,0:T(8,128)S(1)}) fusion(bf16[1024,1024]{1,0:T(8,128)(2,1)S(1)} %get-tuple-element.8, f32[1024]{0:T(1024)S(1)} %bitcast.14, bf16[1024,1024]{1,0:T(8,128)(2,1)S(1)} %get-tuple-element.6, f32[1024]{0:T(1024)S(1)} %bitcast.13), kind=kOutput, calls=%fused_computation.14 | convolution fusion | flops 2155871232 | bytes 8398848 | tf_op jit(solution)/shard_map/dot_general | solution.py:140
  7.8 0.0 copy-start
  7.8 24.7 %all_to_all.45.parts_ref = bf16[64,8,128]{2,1,0:T(8,128)(2,1)S(1)} all-to-all(bf16[64,8,128]{2,1,0:T(8,128)(2,1)S(1)} %broadcast_in_dim.6), channel_id=1, replica_groups=mesh['ylo'=2,'zhi'=4,'zlo'=2,'x'=4,'yhi'=4,'core'=2] {'ylo','zhi','zlo',..., dimensions={0} | all-to-all | bytes 262144 | tf_op jit(solution)/shard_map/all_to_all | solution.py:27
  32.5 0.4 shard_map.42
  32.9 11.1 %all_to_all.46.parts_ref = f32[8,8,128]{2,1,0:T(8,128)S(1)} all-to-all(f32[8,8,128]{2,1,0:T(8,128)S(1)} %shard_map.42), channel_id=1, replica_groups=mesh['ylo'=2,'zhi'=4,'zlo'=2,'x'=4,'yhi'=4,'core'=2] {'yhi','core'}, dimensions={0} | all-to-all | bytes 65536 | tf_op jit(solution)/shard_map/all_to_all | solution.py:27
  44.0 0.4 shard_map.43
  44.3 15.0 %all_to_all.47.parts_ref = bf16[64,8,128]{2,1,0:T(8,128)(2,1)S(1)} all-to-all(bf16[64,8,128]{2,1,0:T(8,128)(2,1)S(1)} %shard_map.43), channel_id=1, replica_groups=mesh['ylo'=2,'zhi'=4,'zlo'=2,'x'=4,'yhi'=4,'core'=2] {'ylo','zhi','zlo',..., dimensions={0} | all-to-all | bytes 262144 | tf_op jit(solution)/shard_map/all_to_all | solution.py:27
  59.4 0.4 shard_map.44
  59.8 10.1 %all_to_all.48.parts_ref = f32[8,8,128]{2,1,0:T(8,128)S(1)} all-to-all(f32[8,8,128]{2,1,0:T(8,128)S(1)} %shard_map.44), channel_id=1, replica_groups=mesh['ylo'=2,'zhi'=4,'zlo'=2,'x'=4,'yhi'=4,'core'=2] {'yhi','core'}, dimensions={0} | all-to-all | bytes 65536 | tf_op jit(solution)/shard_map/all_to_all | solution.py:27
  70.0 0.4 shard_map.45
  70.3 16.4 %all_to_all.49.parts_ref = f32[64,8,128]{2,1,0:T(8,128)S(1)} all-to-all(f32[64,8,128]{2,1,0:T(8,128)S(1)} %shard_map.45), channel_id=1, replica_groups=mesh['ylo'=2,'zhi'=4,'zlo'=2,'x'=4,'yhi'=4,'core'=2] {'ylo','zhi','zlo',..., dimensions={0} | all-to-all | bytes 524288 | tf_op jit(solution)/shard_map/all_to_all | solution.py:27
  86.8 1.0 shard_map.46
  87.8 6.6 %all-to-all-start.5 = ((f32[8,8,128]{2,1,0:T(8,128)}), f32[8,8,128]{2,1,0:T(8,128)S(1)}, u32[]{:S(2)}, u32[]{:S(2)}) async-start(f32[8,8,128]{2,1,0:T(8,128)} %shard_map.46), calls=%async_computation.5 | async-start | bytes 65536 | tf_op jit(solution)/shard_map/all_to_all | solution.py:27
  94.4 0.1 reduce_sum.59
  94.5 4.2 %all-to-all-done.5 = f32[8,8,128]{2,1,0:T(8,128)S(1)} async-done(((f32[8,8,128]{2,1,0:T(8,128)}), f32[8,8,128]{2,1,0:T(8,128)S(1)}, u32[]{:S(2)}, u32[]{:S(2)}) %all-to-all-start.5) | async-done | bytes 32800 | tf_op jit(solution)/shard_map/all_to_all | solution.py:27
  98.7 2.6 %multiply_convert_fusion = bf16[1024,1024]{1,0:T(8,128)(2,1)S(1)} fusion(f32[1024,1024]{1,0:T(8,128)} %copy-done, f32[1024]{0:T(1024)S(1)} %divide_bitcast_fusion, f32[1024]{0:T(1024)S(1)} %multiply_bitcast_fusion), kind=kLoop, calls=%fused_computation | loop fusion | flops 3145728 | bytes 6299648 | tf_op jit(solution)/shard_map/convert_element_type | solution.py:172
  101.3 0.0 copy-start.3
  101.3 2.4 %convolution_convert_fusion = bf16[1024,1024]{1,0:T(8,128)(2,1)S(1)} fusion(bf16[1024,1024]{1,0:T(8,128)(2,1)S(1)} %multiply_convert_fusion, bf16[1024,1024]{1,0:T(8,128)(2,1)S(1)} %get-tuple-element.6), kind=kOutput, calls=%fused_computation.6 | convolution fusion | flops 2148532224 | bytes 6291456 | tf_op jit(solution)/shard_map/dot_general | solution.py:174
  103.7 32.3 %all_to_all.50 = bf16[16,64,1024]{2,1,0:T(8,128)(2,1)S(1)} all-to-all(bf16[16,64,1024]{2,1,0:T(8,128)(2,1)S(1)} %bitcast.16), channel_id=1, replica_groups=mesh['ylo'=2,'zhi'=4,'zlo'=2,'x'=4,'yhi'=4,'core'=2] {'ylo','zlo','x'}, dimensions={0} | all-to-all | bytes 4194304 | tf_op jit(solution)/shard_map/all_to_all | solution.py:27
  136.0 0.4 reduce_sum.60
  136.4 0.1 broadcast_in_dim.7
  136.5 17.8 %all_to_all.51 = bf16[4,64,1024]{2,1,0:T(8,128)(2,1)S(1)} all-to-all(bf16[4,64,1024]{2,1,0:T(8,128)(2,1)S(1)} %broadcast_in_dim.7), channel_id=1, replica_groups=mesh['ylo'=2,'zhi'=4,'zlo'=2,'x'=4,'yhi'=4,'core'=2] {'zhi'}, dimensions={0} | all-to-all | bytes 1048576 | tf_op jit(solution)/shard_map/all_to_all | solution.py:27
  154.3 0.1 convert_reduce_fusion
  154.4 0.1 multiply_reduce_fusion
  154.5 0.1 divide_convert_fusion
  154.7 0.3 broadcast_in_dim.8
  154.9 29.3 %all_to_all.52 = bf16[16,64,1024]{2,1,0:T(8,128)(2,1)S(1)} all-to-all(bf16[16,64,1024]{2,1,0:T(8,128)(2,1)S(1)} %broadcast_in_dim.8), channel_id=1, replica_groups=mesh['ylo'=2,'zhi'=4,'zlo'=2,'x'=4,'yhi'=4,'core'=2] {'ylo','zlo','x'}, dimensions={0} | all-to-all | bytes 4194304 | tf_op jit(solution)/shard_map/all_to_all | solution.py:27
  184.2 1.3 copy.5
  (8 shorter events, 0.1 us)
Async XLA Ops:
  0.6 1.6 copy-start.1
  2.2 1.6 copy-start.2
  7.8 79.0 %copy-start = (f32[1024,1024]{1,0:T(8,128)}, f32[1024,1024]{1,0:T(8,128)S(1)}, u32[]{:S(2)}) copy-start(f32[1024,1024]{1,0:T(8,128)S(1)} %get-tuple-element.11.kernel_ref) | copy-start | bytes 12582916
  87.8 10.9 %all-to-all-start.5 = ((f32[8,8,128]{2,1,0:T(8,128)}), f32[8,8,128]{2,1,0:T(8,128)S(1)}, u32[]{:S(2)}, u32[]{:S(2)}) async-start(f32[8,8,128]{2,1,0:T(8,128)} %shard_map.46), calls=%async_computation.5 | async-start | bytes 65536 | tf_op jit(solution)/shard_map/all_to_all | solution.py:27
  101.3 2.4 %copy-start.3 = (bf16[1024,1024]{1,0:T(8,128)(2,1)}, bf16[1024,1024]{1,0:T(8,128)(2,1)S(1)}, u32[]{:S(2)}) copy-start(bf16[1024,1024]{1,0:T(8,128)(2,1)S(1)} %multiply_convert_fusion) | copy-start | bytes 6291460

commit v4 on v3

--- a/solution.py
+++ b/solution.py
@@ -91,7 +91,7 @@
         in_specs=[whole, whole],
         out_specs=(vmem,) * 4,
         scratch_shapes=[pltpu.SemaphoreType.DMA((2 * halves,))],
-        compiler_params=pltpu.CompilerParams(vmem_limit_bytes=40 * 1024 * 1024),
+        compiler_params=pltpu.CompilerParams(vmem_limit_bytes=48 * 1024 * 1024),
         cost_estimate=pl.CostEstimate(
             flops=4 * embeddings.size, bytes_accessed=8 * embeddings.size, transcendentals=0
         ),
@@ -103,8 +103,10 @@
     out_ref[...] = jnp.broadcast_to(block[None], out_ref.shape)
 
 
-def row_body(scale, kernel_ref, parts_ref, out_ref):
+def row_body(scale, kernel_ref, parts_ref, out_ref, *col_ref):
     col_scale = 1.0 / (scale * jnp.sum(parts_ref[...].astype(jnp.float32), axis=0))
+    for ref in col_ref:
+        ref[...] = col_scale
     lines = []
     for rows in blocks_of(kernel_ref.shape[0]):
         total = None
@@ -149,15 +151,19 @@
     first = jnp.sum(kernel, axis=0).reshape(line_protos).astype(jnp.bfloat16)
     col_parts = everyone(first, ROWS)
     for step in range(ITERS):
-        row_sums = on_chip(
+        last = step == ITERS - 1
+        row_sums, *col_scale = on_chip(
             functools.partial(row_body, proto_count),
-            jax.ShapeDtypeStruct((count(PROTOS), *line_rows), jnp.float32),
+            (
+                jax.ShapeDtypeStruct((count(PROTOS), *line_rows), jnp.float32),
+                *[jax.ShapeDtypeStruct(line_protos, jnp.float32)] * last,
+            ),
             (kernel, col_parts),
             work,
             2 * work,
         )
         row_parts = exchange(row_sums, PROTOS)
-        if step < ITERS - 1:
+        if not last:
             kind = jnp.float32 if step == ITERS - 2 else jnp.bfloat16
             col_sums = on_chip(
                 functools.partial(col_body, row_count),
@@ -167,7 +173,7 @@
                 2 * work,
             )
             col_parts = exchange(col_sums, ROWS)
-    col_scale = (1.0 / (proto_count * jnp.sum(col_parts, axis=0))).reshape(1, protos)
+    col_scale = col_scale[0].reshape(1, protos)
     row_scale = (1.0 / (row_count * jnp.sum(row_parts, axis=0))).reshape(rows, 1)
     codes = (row_count * proto_count * row_scale * kernel * col_scale).astype(jnp.bfloat16)
     feature_width = embeddings.shape[1]

time: 189 us -> 185 us (0.979)
  blocking collectives: 157 us -> 167 us
  starting transfers between devices: 6.61 us -> 0 us
  waiting for transfers between devices: 4.18 us -> 0 us
  local copies, waits for them, and re-layouts: 4.82 us -> 1.65 us
    all_to_all x8 -> x9, blocking collectives: 157 us -> 167 us  [exchange(): return lax.all_to_all(blocks, axes, 0, 0, tiled=True)]
    all_to_all x1 -> x0, starting transfers between devices: 6.61 us -> none  [exchange(): return lax.all_to_all(blocks, axes, 0, 0, tiled=True)]
    all_to_all x1 -> x0, waiting for transfers between devices: 4.18 us -> none  [exchange(): return lax.all_to_all(blocks, axes, 0, 0, tiled=True)]
    unnamed x9 -> x5, local copies, waits for them, and re-layouts: 4.5 us -> 1.33 us
  transfers between devices with their start and end apart: 1 -> 0, of which waited for: 1 -> 0; matrix products, arithmetic and copies ran while one was open for 0% -> 0% of each run, Pallas kernels for 0% -> 0%
where the time goes in v4:
time: 185 us; the launch traced here: 182 us
  blocking collectives  167 us (90%)
  matrix products  4.91 us (3%)
  Pallas kernels  4.5 us (2%)
  other arithmetic  3.32 us (2%)
    all_to_all x9, blocking collectives, exchange(): return lax.all_to_all(blocks, axes, 0, 0, tiled=True)  167 us

profile of v4, /device:TPU:56, one launch (start us, length us, event | category | flops | bytes accessed | tf_op | source)
XLA Modules:
  0.0 181.9 jit_solution(83425161328321199)
XLA Ops:
  0.6 2.5 %shard_map.41 = (bf16[1024,1024]{1,0:T(8,128)(2,1)S(1)}, bf16[1024,1024]{1,0:T(8,128)(2,1)S(1)}, f32[8,128]{1,0:T(8,128)S(1)}, f32[8,128]{1,0:T(8,128)S(1)}) custom-call(bf16[1024,1024]{1,0:T(8,128)(2,1)} %rows_in.1, bf16[1024,1024]{1,0:T(8,128)(2,1)} %protos_in.1), custom_call_target="tpu_custom_call" | custom-call | flops 4194304 | bytes 8388608 | tf_op jit(solution)/shard_map/pallas_call | solution.py:85
  3.1 2.5 %fusion.2 = (bf16[1024]{0:T(1024)(128)(2,1)S(1)}, f32[1024,1024]{1,0:T(8,128)S(1)}) fusion(bf16[1024,1024]{1,0:T(8,128)(2,1)S(1)} %get-tuple-element.10, f32[1024]{0:T(1024)S(1)} %bitcast.14, bf16[1024,1024]{1,0:T(8,128)(2,1)S(1)} %get-tuple-element.8, f32[1024]{0:T(1024)S(1)} %bitcast.13), kind=kOutput, calls=%fused_computation.13 | convolution fusion | flops 2155871232 | bytes 8398848 | tf_op jit(solution)/shard_map/dot_general | solution.py:142
  5.6 0.0 copy-start
  5.7 24.7 %all_to_all.45.parts_ref = bf16[64,8,128]{2,1,0:T(8,128)(2,1)S(1)} all-to-all(bf16[64,8,128]{2,1,0:T(8,128)(2,1)S(1)} %broadcast_in_dim.6), channel_id=1, replica_groups=mesh['ylo'=2,'zhi'=4,'zlo'=2,'x'=4,'yhi'=4,'core'=2] {'ylo','zhi','zlo',..., dimensions={0} | all-to-all | bytes 262144 | tf_op jit(solution)/shard_map/all_to_all | solution.py:27
  30.3 0.4 shard_map.42
  30.8 11.1 %all_to_all.46.parts_ref = f32[8,8,128]{2,1,0:T(8,128)S(1)} all-to-all(f32[8,8,128]{2,1,0:T(8,128)S(1)} %shard_map.42), channel_id=1, replica_groups=mesh['ylo'=2,'zhi'=4,'zlo'=2,'x'=4,'yhi'=4,'core'=2] {'yhi','core'}, dimensions={0} | all-to-all | bytes 65536 | tf_op jit(solution)/shard_map/all_to_all | solution.py:27
  41.8 0.4 shard_map.43
  42.2 15.0 %all_to_all.47.parts_ref = bf16[64,8,128]{2,1,0:T(8,128)(2,1)S(1)} all-to-all(bf16[64,8,128]{2,1,0:T(8,128)(2,1)S(1)} %shard_map.43), channel_id=1, replica_groups=mesh['ylo'=2,'zhi'=4,'zlo'=2,'x'=4,'yhi'=4,'core'=2] {'ylo','zhi','zlo',..., dimensions={0} | all-to-all | bytes 262144 | tf_op jit(solution)/shard_map/all_to_all | solution.py:27
  57.3 0.4 shard_map.44
  57.7 10.1 %all_to_all.48.parts_ref = f32[8,8,128]{2,1,0:T(8,128)S(1)} all-to-all(f32[8,8,128]{2,1,0:T(8,128)S(1)} %shard_map.44), channel_id=1, replica_groups=mesh['ylo'=2,'zhi'=4,'zlo'=2,'x'=4,'yhi'=4,'core'=2] {'yhi','core'}, dimensions={0} | all-to-all | bytes 65536 | tf_op jit(solution)/shard_map/all_to_all | solution.py:27
  67.8 0.4 shard_map.45
  68.2 16.4 %all_to_all.49.parts_ref = f32[64,8,128]{2,1,0:T(8,128)S(1)} all-to-all(f32[64,8,128]{2,1,0:T(8,128)S(1)} %shard_map.45), channel_id=1, replica_groups=mesh['ylo'=2,'zhi'=4,'zlo'=2,'x'=4,'yhi'=4,'core'=2] {'ylo','zhi','zlo',..., dimensions={0} | all-to-all | bytes 524288 | tf_op jit(solution)/shard_map/all_to_all | solution.py:27
  84.6 0.0 copy-done
  84.6 0.4 shard_map.46
  85.1 10.0 %all_to_all.50 = f32[8,8,128]{2,1,0:T(8,128)S(1)} all-to-all(f32[8,8,128]{2,1,0:T(8,128)S(1)} %get-tuple-element.12), channel_id=1, replica_groups=mesh['ylo'=2,'zhi'=4,'zlo'=2,'x'=4,'yhi'=4,'core'=2] {'yhi','core'}, dimensions={0} | all-to-all | bytes 65536 | tf_op jit(solution)/shard_map/all_to_all | solution.py:27
  95.0 2.6 %multiply_convert_fusion = bf16[1024,1024]{1,0:T(8,128)(2,1)S(1)} fusion(f32[1024,1024]{1,0:T(8,128)} %copy-done, f32[1024]{0:T(1024)S(1)} %bitcast.12, f32[1024]{0:T(1024)S(1)} %multiply_bitcast_fusion), kind=kLoop, calls=%fused_computation | loop fusion | flops 3145728 | bytes 6299648 | tf_op jit(solution)/shard_map/convert_element_type | solution.py:178
  97.7 0.0 copy-start.1
  97.7 2.4 %convolution_convert_fusion = bf16[1024,1024]{1,0:T(8,128)(2,1)S(1)} fusion(bf16[1024,1024]{1,0:T(8,128)(2,1)S(1)} %multiply_convert_fusion, bf16[1024,1024]{1,0:T(8,128)(2,1)S(1)} %get-tuple-element.8), kind=kOutput, calls=%fused_computation.6 | convolution fusion | flops 2148532224 | bytes 6291456 | tf_op jit(solution)/shard_map/dot_general | solution.py:180
  100.1 0.0 copy-done.1
  100.1 32.3 %all_to_all.51 = bf16[16,64,1024]{2,1,0:T(8,128)(2,1)S(1)} all-to-all(bf16[16,64,1024]{2,1,0:T(8,128)(2,1)S(1)} %bitcast.16), channel_id=1, replica_groups=mesh['ylo'=2,'zhi'=4,'zlo'=2,'x'=4,'yhi'=4,'core'=2] {'ylo','zlo','x'}, dimensions={0} | all-to-all | bytes 4194304 | tf_op jit(solution)/shard_map/all_to_all | solution.py:27
  132.4 0.4 reduce_sum.50
  132.8 0.1 broadcast_in_dim.7
  132.9 17.8 %all_to_all.52 = bf16[4,64,1024]{2,1,0:T(8,128)(2,1)S(1)} all-to-all(bf16[4,64,1024]{2,1,0:T(8,128)(2,1)S(1)} %broadcast_in_dim.7), channel_id=1, replica_groups=mesh['ylo'=2,'zhi'=4,'zlo'=2,'x'=4,'yhi'=4,'core'=2] {'zhi'}, dimensions={0} | all-to-all | bytes 1048576 | tf_op jit(solution)/shard_map/all_to_all | solution.py:27
  150.7 0.1 convert_reduce_fusion
  150.8 0.1 multiply_reduce_fusion
  150.9 0.1 divide_convert_fusion
  151.0 0.3 broadcast_in_dim.8
  151.3 29.3 %all_to_all.53 = bf16[16,64,1024]{2,1,0:T(8,128)(2,1)S(1)} all-to-all(bf16[16,64,1024]{2,1,0:T(8,128)(2,1)S(1)} %broadcast_in_dim.8), channel_id=1, replica_groups=mesh['ylo'=2,'zhi'=4,'zlo'=2,'x'=4,'yhi'=4,'core'=2] {'ylo','zlo','x'}, dimensions={0} | all-to-all | bytes 4194304 | tf_op jit(solution)/shard_map/all_to_all | solution.py:27
  180.6 1.3 copy.5
  (4 shorter events, 0.0 us)
Async XLA Ops:
  5.6 79.0 %copy-start = (f32[1024,1024]{1,0:T(8,128)}, f32[1024,1024]{1,0:T(8,128)S(1)}, u32[]{:S(2)}) copy-start(f32[1024,1024]{1,0:T(8,128)S(1)} %get-tuple-element.15.kernel_ref) | copy-start | bytes 12582916
  97.7 2.4 %copy-start.1 = (bf16[1024,1024]{1,0:T(8,128)(2,1)}, bf16[1024,1024]{1,0:T(8,128)(2,1)S(1)}, u32[]{:S(2)}) copy-start(bf16[1024,1024]{1,0:T(8,128)(2,1)S(1)} %multiply_convert_fusion) | copy-start | bytes 6291460

commit v5 on v4

--- a/solution.py
+++ b/solution.py
@@ -132,6 +132,43 @@
 
 def unit(values, inverse):
     return (values.astype(jnp.float32) * inverse.reshape(-1, 1)).astype(jnp.bfloat16)
+
+
+def codes_body(scale, mass, kernel_ref, parts_ref, col_ref, codes_ref):
+    row_scale = mass / (scale * jnp.sum(parts_ref[...], axis=0))
+    col_scale = col_ref[...]
+    for r, rows in enumerate(blocks_of(kernel_ref.shape[0])):
+        turned = down_rows(row_scale[r : r + 1, :])
+        for k, lanes in enumerate(blocks_of(kernel_ref.shape[1])):
+            tile = turned * kernel_ref[rows, lanes] * col_scale[k : k + 1, :]
+            codes_ref[rows, lanes] = tile.astype(jnp.bfloat16)
+
+
+def write_body(parts, source, target, sems):
+    size = source.shape[0] // parts
+    copies = []
+    for part in range(parts):
+        rows = pl.ds(part * size, size)
+        copy = pltpu.make_async_copy(source.at[rows, :], target.at[rows, :], sems.at[part])
+        copy.start()
+        copies.append(copy)
+    for copy in copies:
+        copy.wait()
+
+
+def write_out(array):
+    parts = 4
+    return pl.pallas_call(
+        functools.partial(write_body, parts),
+        out_shape=jax.ShapeDtypeStruct(array.shape, array.dtype),
+        in_specs=[pl.BlockSpec(memory_space=pltpu.VMEM)],
+        out_specs=pl.BlockSpec(memory_space=pl.ANY),
+        scratch_shapes=[pltpu.SemaphoreType.DMA((parts,))],
+        compiler_params=pltpu.CompilerParams(vmem_limit_bytes=8 * 1024 * 1024),
+        cost_estimate=pl.CostEstimate(
+            flops=0, bytes_accessed=4 * array.size, transcendentals=0
+        ),
+    )(array)
 
 
 def body(embeddings, prototypes):
@@ -164,22 +201,28 @@
         )
         row_parts = exchange(row_sums, PROTOS)
         if not last:
-            kind = jnp.float32 if step == ITERS - 2 else jnp.bfloat16
             col_sums = on_chip(
                 functools.partial(col_body, row_count),
-                jax.ShapeDtypeStruct((count(ROWS), *line_protos), kind),
+                jax.ShapeDtypeStruct((count(ROWS), *line_protos), jnp.bfloat16),
                 (kernel, row_parts),
                 work,
                 2 * work,
             )
             col_parts = exchange(col_sums, ROWS)
-    col_scale = col_scale[0].reshape(1, protos)
-    row_scale = (1.0 / (row_count * jnp.sum(row_parts, axis=0))).reshape(rows, 1)
-    codes = (row_count * proto_count * row_scale * kernel * col_scale).astype(jnp.bfloat16)
+    mass = row_count * proto_count
+    early_codes = on_chip(
+        functools.partial(codes_body, row_count, mass),
+        jax.ShapeDtypeStruct(kernel.shape, jnp.bfloat16),
+        (kernel, row_parts, col_scale[0]),
+        work,
+        3 * work,
+    )
     feature_width = embeddings.shape[1]
     term = lax.dot_general(
-        codes, embeddings, (((0,), (0,)), ((), ())), preferred_element_type=jnp.float32
+        early_codes, embeddings, (((0,), (0,)), ((), ())), preferred_element_type=jnp.float32
     ).astype(jnp.bfloat16)
+    term, early_codes = lax.optimization_barrier((term, early_codes))
+    term, codes = lax.optimization_barrier((term, write_out(early_codes)))
     near = exchange(term.reshape(count(NEAR), -1, feature_width), NEAR)
     near = jnp.sum(near.astype(jnp.float32), axis=0).astype(jnp.bfloat16)
     sums = jnp.sum(everyone(near, FAR).astype(jnp.float32), axis=0)

time: 185 us -> 181 us (0.978)
  blocking collectives: 167 us -> 164 us
  other arithmetic: 3.32 us -> 0.7 us
  Pallas kernels: 4.5 us -> 6.4 us
    all_to_all x9, blocking collectives: 167 us -> 164 us  [exchange(): return lax.all_to_all(blocks, axes, 0, 0, tiled=True)]
    convert_element_type x1 -> x0, other arithmetic: 2.6 us -> none  [body(): (row_count * proto_count * row_scale * kernel * col_scale).astype(jnp.bfl...]
where the time goes in v5:
time: 181 us; the launch traced here: 178 us
  blocking collectives  164 us (91%)
  Pallas kernels  6.4 us (4%)
  matrix products  4.95 us (3%)
    all_to_all x9, blocking collectives, exchange(): return lax.all_to_all(blocks, axes, 0, 0, tiled=True)  164 us

profile of v5, /device:TPU:56, one launch (start us, length us, event | category | flops | bytes accessed | tf_op | source)
XLA Modules:
  0.0 178.4 jit_solution(11793075338831539254)
XLA Ops:
  0.6 2.5 %shard_map.41 = (bf16[1024,1024]{1,0:T(8,128)(2,1)S(1)}, bf16[1024,1024]{1,0:T(8,128)(2,1)S(1)}, f32[8,128]{1,0:T(8,128)S(1)}, f32[8,128]{1,0:T(8,128)S(1)}) custom-call(bf16[1024,1024]{1,0:T(8,128)(2,1)} %rows_in.1, bf16[1024,1024]{1,0:T(8,128)(2,1)} %protos_in.1), custom_call_target="tpu_custom_call" | custom-call | flops 4194304 | bytes 8388608 | tf_op jit(solution)/shard_map/pallas_call | solution.py:85
  3.1 2.5 %fusion.2 = (bf16[1024]{0:T(1024)(128)(2,1)S(1)}, f32[1024,1024]{1,0:T(8,128)S(1)}) fusion(bf16[1024,1024]{1,0:T(8,128)(2,1)S(1)} %get-tuple-element.14, f32[1024]{0:T(1024)S(1)} %bitcast.10, bf16[1024,1024]{1,0:T(8,128)(2,1)S(1)} %get-tuple-element.12, f32[1024]{0:T(1024)S(1)} %bitcast.9), kind=kOutput, calls=%fused_computation.11 | convolution fusion | flops 2155871232 | bytes 8398848 | tf_op jit(solution)/shard_map/dot_general | solution.py:179
  5.7 24.7 %all_to_all.45.parts_ref = bf16[64,8,128]{2,1,0:T(8,128)(2,1)S(1)} all-to-all(bf16[64,8,128]{2,1,0:T(8,128)(2,1)S(1)} %broadcast_in_dim.6), channel_id=1, replica_groups=mesh['ylo'=2,'zhi'=4,'zlo'=2,'x'=4,'yhi'=4,'core'=2] {'ylo','zhi','zlo',..., dimensions={0} | all-to-all | bytes 262144 | tf_op jit(solution)/shard_map/all_to_all | solution.py:27
  30.4 0.4 shard_map.42
  30.8 11.1 %all_to_all.46.parts_ref = f32[8,8,128]{2,1,0:T(8,128)S(1)} all-to-all(f32[8,8,128]{2,1,0:T(8,128)S(1)} %shard_map.42), channel_id=1, replica_groups=mesh['ylo'=2,'zhi'=4,'zlo'=2,'x'=4,'yhi'=4,'core'=2] {'yhi','core'}, dimensions={0} | all-to-all | bytes 65536 | tf_op jit(solution)/shard_map/all_to_all | solution.py:27
  41.8 0.4 shard_map.43
  42.2 15.0 %all_to_all.47.parts_ref = bf16[64,8,128]{2,1,0:T(8,128)(2,1)S(1)} all-to-all(bf16[64,8,128]{2,1,0:T(8,128)(2,1)S(1)} %shard_map.43), channel_id=1, replica_groups=mesh['ylo'=2,'zhi'=4,'zlo'=2,'x'=4,'yhi'=4,'core'=2] {'ylo','zhi','zlo',..., dimensions={0} | all-to-all | bytes 262144 | tf_op jit(solution)/shard_map/all_to_all | solution.py:27
  57.3 0.4 shard_map.44
  57.7 10.1 %all_to_all.48.parts_ref = f32[8,8,128]{2,1,0:T(8,128)S(1)} all-to-all(f32[8,8,128]{2,1,0:T(8,128)S(1)} %shard_map.44), channel_id=1, replica_groups=mesh['ylo'=2,'zhi'=4,'zlo'=2,'x'=4,'yhi'=4,'core'=2] {'yhi','core'}, dimensions={0} | all-to-all | bytes 65536 | tf_op jit(solution)/shard_map/all_to_all | solution.py:27
  67.8 0.4 shard_map.45
  68.2 15.0 %all_to_all.49.parts_ref = bf16[64,8,128]{2,1,0:T(8,128)(2,1)S(1)} all-to-all(bf16[64,8,128]{2,1,0:T(8,128)(2,1)S(1)} %shard_map.45), channel_id=1, replica_groups=mesh['ylo'=2,'zhi'=4,'zlo'=2,'x'=4,'yhi'=4,'core'=2] {'ylo','zhi','zlo',..., dimensions={0} | all-to-all | bytes 262144 | tf_op jit(solution)/shard_map/all_to_all | solution.py:27
  83.2 0.4 shard_map.46
  83.7 10.1 %all_to_all.50.parts_ref = f32[8,8,128]{2,1,0:T(8,128)S(1)} all-to-all(f32[8,8,128]{2,1,0:T(8,128)S(1)} %get-tuple-element.16), channel_id=1, replica_groups=mesh['ylo'=2,'zhi'=4,'zlo'=2,'x'=4,'yhi'=4,'core'=2] {'yhi','core'}, dimensions={0} | all-to-all | bytes 65536 | tf_op jit(solution)/shard_map/all_to_all | solution.py:27
  93.8 0.6 shard_map.47.source
  94.4 2.4 %convolution_convert_fusion = bf16[1024,1024]{1,0:T(8,128)(2,1)S(1)} fusion(bf16[1024,1024]{1,0:T(8,128)(2,1)S(1)} %shard_map.47.source, bf16[1024,1024]{1,0:T(8,128)(2,1)S(1)} %get-tuple-element.12), kind=kOutput, calls=%fused_computation.5 | convolution fusion | flops 2148532224 | bytes 6291456 | tf_op jit(solution)/shard_map/dot_general | solution.py:221
  96.8 1.3 shard_map.48
  98.2 31.4 %all_to_all.51 = bf16[16,64,1024]{2,1,0:T(8,128)(2,1)S(1)} all-to-all(bf16[16,64,1024]{2,1,0:T(8,128)(2,1)S(1)} %bitcast.12), channel_id=1, replica_groups=mesh['ylo'=2,'zhi'=4,'zlo'=2,'x'=4,'yhi'=4,'core'=2] {'ylo','zlo','x'}, dimensions={0} | all-to-all | bytes 4194304 | tf_op jit(solution)/shard_map/all_to_all | solution.py:27
  129.6 0.4 reduce_sum.40
  130.0 0.1 broadcast_in_dim.7
  130.0 17.2 %all_to_all.52 = bf16[4,64,1024]{2,1,0:T(8,128)(2,1)S(1)} all-to-all(bf16[4,64,1024]{2,1,0:T(8,128)(2,1)S(1)} %broadcast_in_dim.7), channel_id=1, replica_groups=mesh['ylo'=2,'zhi'=4,'zlo'=2,'x'=4,'yhi'=4,'core'=2] {'zhi'}, dimensions={0} | all-to-all | bytes 1048576 | tf_op jit(solution)/shard_map/all_to_all | solution.py:27
  147.2 0.1 convert_reduce_fusion
  147.3 0.1 multiply_reduce_fusion
  147.4 0.1 divide_convert_fusion
  147.6 0.3 broadcast_in_dim.8
  147.8 29.3 %all_to_all.53 = bf16[16,64,1024]{2,1,0:T(8,128)(2,1)S(1)} all-to-all(bf16[16,64,1024]{2,1,0:T(8,128)(2,1)S(1)} %broadcast_in_dim.8), channel_id=1, replica_groups=mesh['ylo'=2,'zhi'=4,'zlo'=2,'x'=4,'yhi'=4,'core'=2] {'ylo','zlo','x'}, dimensions={0} | all-to-all | bytes 4194304 | tf_op jit(solution)/shard_map/all_to_all | solution.py:27
  177.1 1.3 copy.5
  (2 shorter events, 0.0 us)

commit v6 on v5

--- a/solution.py
+++ b/solution.py
@@ -11,7 +11,7 @@
 LANES = 128
 ROWS = ("ylo", "zhi", "zlo", "x")
 PROTOS = ("yhi", "core")
-NEAR = ("ylo", "zlo", "x")
+NEAR = ("x", "zlo", "ylo")
 FAR = ("zhi",)
 SIZES = {"ylo": 2, "zhi": 4, "zlo": 2, "x": 4, "yhi": 4, "core": 2}
 

time: 181 us -> 182 us (level)
  no operation moved by 1% of the time
where the time goes in v6:
time: 182 us; the launch traced here: 179 us
  blocking collectives  164 us (90%)
  Pallas kernels  6.4 us (4%)
  matrix products  4.95 us (3%)
    all_to_all x9, blocking collectives, exchange(): return lax.all_to_all(blocks, axes, 0, 0, tiled=True)  164 us

profile of v6, /device:TPU:56, one launch (start us, length us, event | category | flops | bytes accessed | tf_op | source)
XLA Modules:
  0.0 178.7 jit_solution(16259682077013505508)
XLA Ops:
  0.6 2.5 %shard_map.41 = (bf16[1024,1024]{1,0:T(8,128)(2,1)S(1)}, bf16[1024,1024]{1,0:T(8,128)(2,1)S(1)}, f32[8,128]{1,0:T(8,128)S(1)}, f32[8,128]{1,0:T(8,128)S(1)}) custom-call(bf16[1024,1024]{1,0:T(8,128)(2,1)} %rows_in.1, bf16[1024,1024]{1,0:T(8,128)(2,1)} %protos_in.1), custom_call_target="tpu_custom_call" | custom-call | flops 4194304 | bytes 8388608 | tf_op jit(solution)/shard_map/pallas_call | solution.py:85
  3.1 2.5 %fusion.2 = (bf16[1024]{0:T(1024)(128)(2,1)S(1)}, f32[1024,1024]{1,0:T(8,128)S(1)}) fusion(bf16[1024,1024]{1,0:T(8,128)(2,1)S(1)} %get-tuple-element.14, f32[1024]{0:T(1024)S(1)} %bitcast.10, bf16[1024,1024]{1,0:T(8,128)(2,1)S(1)} %get-tuple-element.12, f32[1024]{0:T(1024)S(1)} %bitcast.9), kind=kOutput, calls=%fused_computation.11 | convolution fusion | flops 2155871232 | bytes 8398848 | tf_op jit(solution)/shard_map/dot_general | solution.py:179
  5.7 24.7 %all_to_all.45.parts_ref = bf16[64,8,128]{2,1,0:T(8,128)(2,1)S(1)} all-to-all(bf16[64,8,128]{2,1,0:T(8,128)(2,1)S(1)} %broadcast_in_dim.6), channel_id=1, replica_groups=mesh['ylo'=2,'zhi'=4,'zlo'=2,'x'=4,'yhi'=4,'core'=2] {'ylo','zhi','zlo',..., dimensions={0} | all-to-all | bytes 262144 | tf_op jit(solution)/shard_map/all_to_all | solution.py:27
  30.4 0.4 shard_map.42
  30.8 11.1 %all_to_all.46.parts_ref = f32[8,8,128]{2,1,0:T(8,128)S(1)} all-to-all(f32[8,8,128]{2,1,0:T(8,128)S(1)} %shard_map.42), channel_id=1, replica_groups=mesh['ylo'=2,'zhi'=4,'zlo'=2,'x'=4,'yhi'=4,'core'=2] {'yhi','core'}, dimensions={0} | all-to-all | bytes 65536 | tf_op jit(solution)/shard_map/all_to_all | solution.py:27
  41.8 0.4 shard_map.43
  42.2 15.0 %all_to_all.47.parts_ref = bf16[64,8,128]{2,1,0:T(8,128)(2,1)S(1)} all-to-all(bf16[64,8,128]{2,1,0:T(8,128)(2,1)S(1)} %shard_map.43), channel_id=1, replica_groups=mesh['ylo'=2,'zhi'=4,'zlo'=2,'x'=4,'yhi'=4,'core'=2] {'ylo','zhi','zlo',..., dimensions={0} | all-to-all | bytes 262144 | tf_op jit(solution)/shard_map/all_to_all | solution.py:27
  57.3 0.4 shard_map.44
  57.7 10.1 %all_to_all.48.parts_ref = f32[8,8,128]{2,1,0:T(8,128)S(1)} all-to-all(f32[8,8,128]{2,1,0:T(8,128)S(1)} %shard_map.44), channel_id=1, replica_groups=mesh['ylo'=2,'zhi'=4,'zlo'=2,'x'=4,'yhi'=4,'core'=2] {'yhi','core'}, dimensions={0} | all-to-all | bytes 65536 | tf_op jit(solution)/shard_map/all_to_all | solution.py:27
  67.8 0.4 shard_map.45
  68.2 15.0 %all_to_all.49.parts_ref = bf16[64,8,128]{2,1,0:T(8,128)(2,1)S(1)} all-to-all(bf16[64,8,128]{2,1,0:T(8,128)(2,1)S(1)} %shard_map.45), channel_id=1, replica_groups=mesh['ylo'=2,'zhi'=4,'zlo'=2,'x'=4,'yhi'=4,'core'=2] {'ylo','zhi','zlo',..., dimensions={0} | all-to-all | bytes 262144 | tf_op jit(solution)/shard_map/all_to_all | solution.py:27
  83.2 0.4 shard_map.46
  83.7 10.1 %all_to_all.50.parts_ref = f32[8,8,128]{2,1,0:T(8,128)S(1)} all-to-all(f32[8,8,128]{2,1,0:T(8,128)S(1)} %get-tuple-element.16), channel_id=1, replica_groups=mesh['ylo'=2,'zhi'=4,'zlo'=2,'x'=4,'yhi'=4,'core'=2] {'yhi','core'}, dimensions={0} | all-to-all | bytes 65536 | tf_op jit(solution)/shard_map/all_to_all | solution.py:27
  93.8 0.6 shard_map.47.source
  94.4 2.4 %convolution_convert_fusion = bf16[1024,1024]{1,0:T(8,128)(2,1)S(1)} fusion(bf16[1024,1024]{1,0:T(8,128)(2,1)S(1)} %shard_map.47.source, bf16[1024,1024]{1,0:T(8,128)(2,1)S(1)} %get-tuple-element.12), kind=kOutput, calls=%fused_computation.5 | convolution fusion | flops 2148532224 | bytes 6291456 | tf_op jit(solution)/shard_map/dot_general | solution.py:221
  96.8 1.3 shard_map.48
  98.2 30.4 %all_to_all.51 = bf16[16,64,1024]{2,1,0:T(8,128)(2,1)S(1)} all-to-all(bf16[16,64,1024]{2,1,0:T(8,128)(2,1)S(1)} %bitcast.12), channel_id=1, replica_groups=mesh['ylo'=2,'zhi'=4,'zlo'=2,'x'=4,'yhi'=4,'core'=2] {'x','zlo','ylo'}, dimensions={0} | all-to-all | bytes 4194304 | tf_op jit(solution)/shard_map/all_to_all | solution.py:27
  128.6 0.4 reduce_sum.40
  129.0 0.1 broadcast_in_dim.7
  129.0 18.3 %all_to_all.52 = bf16[4,64,1024]{2,1,0:T(8,128)(2,1)S(1)} all-to-all(bf16[4,64,1024]{2,1,0:T(8,128)(2,1)S(1)} %broadcast_in_dim.7), channel_id=1, replica_groups=mesh['ylo'=2,'zhi'=4,'zlo'=2,'x'=4,'yhi'=4,'core'=2] {'zhi'}, dimensions={0} | all-to-all | bytes 1048576 | tf_op jit(solution)/shard_map/all_to_all | solution.py:27
  147.3 0.1 convert_reduce_fusion
  147.4 0.1 multiply_reduce_fusion
  147.5 0.1 divide_convert_fusion
  147.6 0.3 broadcast_in_dim.8
  147.9 29.5 %all_to_all.53 = bf16[16,64,1024]{2,1,0:T(8,128)(2,1)S(1)} all-to-all(bf16[16,64,1024]{2,1,0:T(8,128)(2,1)S(1)} %broadcast_in_dim.8), channel_id=1, replica_groups=mesh['ylo'=2,'zhi'=4,'zlo'=2,'x'=4,'yhi'=4,'core'=2] {'x','zlo','ylo'}, dimensions={0} | all-to-all | bytes 4194304 | tf_op jit(solution)/shard_map/all_to_all | solution.py:27
  177.4 1.3 copy.5
  (2 shorter events, 0.0 us)

commit v7 on v6

--- a/solution.py
+++ b/solution.py
@@ -12,6 +12,7 @@
 ROWS = ("ylo", "zhi", "zlo", "x")
 PROTOS = ("yhi", "core")
 NEAR = ("x", "zlo", "ylo")
+BACK = ("ylo", "zlo", "x")
 FAR = ("zhi",)
 SIZES = {"ylo": 2, "zhi": 4, "zlo": 2, "x": 4, "yhi": 4, "core": 2}
 
@@ -228,7 +229,9 @@
     sums = jnp.sum(everyone(near, FAR).astype(jnp.float32), axis=0)
     squares = jnp.sum(sums * sums, axis=1, keepdims=True)
     scaled = (sums / jnp.sqrt(squares / feature_width + 1e-06)).astype(jnp.bfloat16)
-    return (codes, everyone(scaled, NEAR).reshape(protos, feature_width))
+    blocks = everyone(scaled, BACK)
+    blocks = blocks.reshape(*(SIZES[axis] for axis in BACK), *scaled.shape)
+    return (codes, jnp.transpose(blocks, (2, 1, 0, 3, 4)).reshape(protos, feature_width))
 
 
 def solution(mesh):

time: 182 us -> 182 us (level)
  no operation moved by 1% of the time
where the time goes in v7:
time: 182 us; the launch traced here: 180 us
  blocking collectives  165 us (91%)
  Pallas kernels  6.4 us (4%)
  matrix products  4.95 us (3%)
    all_to_all x9, blocking collectives, exchange(): return lax.all_to_all(blocks, axes, 0, 0, tiled=True)  165 us

profile of v7, /device:TPU:56, one launch (start us, length us, event | category | flops | bytes accessed | tf_op | source)
XLA Modules:
  0.0 179.7 jit_solution(6471366657484471424)
XLA Ops:
  0.6 2.5 %shard_map.41 = (bf16[1024,1024]{1,0:T(8,128)(2,1)S(1)}, bf16[1024,1024]{1,0:T(8,128)(2,1)S(1)}, f32[8,128]{1,0:T(8,128)S(1)}, f32[8,128]{1,0:T(8,128)S(1)}) custom-call(bf16[1024,1024]{1,0:T(8,128)(2,1)} %rows_in.1, bf16[1024,1024]{1,0:T(8,128)(2,1)} %protos_in.1), custom_call_target="tpu_custom_call" | custom-call | flops 4194304 | bytes 8388608 | tf_op jit(solution)/shard_map/pallas_call | solution.py:86
  3.1 2.5 %fusion.2 = (bf16[1024]{0:T(1024)(128)(2,1)S(1)}, f32[1024,1024]{1,0:T(8,128)S(1)}) fusion(bf16[1024,1024]{1,0:T(8,128)(2,1)S(1)} %get-tuple-element.14, f32[1024]{0:T(1024)S(1)} %bitcast.13, bf16[1024,1024]{1,0:T(8,128)(2,1)S(1)} %get-tuple-element.12, f32[1024]{0:T(1024)S(1)} %bitcast.12), kind=kOutput, calls=%fused_computation.11 | convolution fusion | flops 2155871232 | bytes 8398848 | tf_op jit(solution)/shard_map/dot_general | solution.py:180
  5.7 24.7 %all_to_all.45.parts_ref = bf16[64,8,128]{2,1,0:T(8,128)(2,1)S(1)} all-to-all(bf16[64,8,128]{2,1,0:T(8,128)(2,1)S(1)} %broadcast_in_dim.6), channel_id=1, replica_groups=mesh['ylo'=2,'zhi'=4,'zlo'=2,'x'=4,'yhi'=4,'core'=2] {'ylo','zhi','zlo',..., dimensions={0} | all-to-all | bytes 262144 | tf_op jit(solution)/shard_map/all_to_all | solution.py:28
  30.4 0.4 shard_map.42
  30.8 11.1 %all_to_all.46.parts_ref = f32[8,8,128]{2,1,0:T(8,128)S(1)} all-to-all(f32[8,8,128]{2,1,0:T(8,128)S(1)} %shard_map.42), channel_id=1, replica_groups=mesh['ylo'=2,'zhi'=4,'zlo'=2,'x'=4,'yhi'=4,'core'=2] {'yhi','core'}, dimensions={0} | all-to-all | bytes 65536 | tf_op jit(solution)/shard_map/all_to_all | solution.py:28
  41.8 0.4 shard_map.43
  42.2 15.0 %all_to_all.47.parts_ref = bf16[64,8,128]{2,1,0:T(8,128)(2,1)S(1)} all-to-all(bf16[64,8,128]{2,1,0:T(8,128)(2,1)S(1)} %shard_map.43), channel_id=1, replica_groups=mesh['ylo'=2,'zhi'=4,'zlo'=2,'x'=4,'yhi'=4,'core'=2] {'ylo','zhi','zlo',..., dimensions={0} | all-to-all | bytes 262144 | tf_op jit(solution)/shard_map/all_to_all | solution.py:28
  57.3 0.4 shard_map.44
  57.7 10.1 %all_to_all.48.parts_ref = f32[8,8,128]{2,1,0:T(8,128)S(1)} all-to-all(f32[8,8,128]{2,1,0:T(8,128)S(1)} %shard_map.44), channel_id=1, replica_groups=mesh['ylo'=2,'zhi'=4,'zlo'=2,'x'=4,'yhi'=4,'core'=2] {'yhi','core'}, dimensions={0} | all-to-all | bytes 65536 | tf_op jit(solution)/shard_map/all_to_all | solution.py:28
  67.8 0.4 shard_map.45
  68.2 15.0 %all_to_all.49.parts_ref = bf16[64,8,128]{2,1,0:T(8,128)(2,1)S(1)} all-to-all(bf16[64,8,128]{2,1,0:T(8,128)(2,1)S(1)} %shard_map.45), channel_id=1, replica_groups=mesh['ylo'=2,'zhi'=4,'zlo'=2,'x'=4,'yhi'=4,'core'=2] {'ylo','zhi','zlo',..., dimensions={0} | all-to-all | bytes 262144 | tf_op jit(solution)/shard_map/all_to_all | solution.py:28
  83.2 0.4 shard_map.46
  83.7 10.1 %all_to_all.50.parts_ref = f32[8,8,128]{2,1,0:T(8,128)S(1)} all-to-all(f32[8,8,128]{2,1,0:T(8,128)S(1)} %get-tuple-element.16), channel_id=1, replica_groups=mesh['ylo'=2,'zhi'=4,'zlo'=2,'x'=4,'yhi'=4,'core'=2] {'yhi','core'}, dimensions={0} | all-to-all | bytes 65536 | tf_op jit(solution)/shard_map/all_to_all | solution.py:28
  93.8 0.6 shard_map.47.source
  94.4 2.4 %convolution_convert_fusion = bf16[1024,1024]{1,0:T(8,128)(2,1)S(1)} fusion(bf16[1024,1024]{1,0:T(8,128)(2,1)S(1)} %shard_map.47.source, bf16[1024,1024]{1,0:T(8,128)(2,1)S(1)} %get-tuple-element.12), kind=kOutput, calls=%fused_computation.5 | convolution fusion | flops 2148532224 | bytes 6291456 | tf_op jit(solution)/shard_map/dot_general | solution.py:222
  96.8 1.3 shard_map.48
  98.2 30.4 %all_to_all.51 = bf16[16,64,1024]{2,1,0:T(8,128)(2,1)S(1)} all-to-all(bf16[16,64,1024]{2,1,0:T(8,128)(2,1)S(1)} %bitcast.16), channel_id=1, replica_groups=mesh['ylo'=2,'zhi'=4,'zlo'=2,'x'=4,'yhi'=4,'core'=2] {'x','zlo','ylo'}, dimensions={0} | all-to-all | bytes 4194304 | tf_op jit(solution)/shard_map/all_to_all | solution.py:28
  128.6 0.4 reduce_sum.40
  129.0 0.1 broadcast_in_dim.7
  129.0 18.3 %all_to_all.52 = bf16[4,64,1024]{2,1,0:T(8,128)(2,1)S(1)} all-to-all(bf16[4,64,1024]{2,1,0:T(8,128)(2,1)S(1)} %broadcast_in_dim.7), channel_id=1, replica_groups=mesh['ylo'=2,'zhi'=4,'zlo'=2,'x'=4,'yhi'=4,'core'=2] {'zhi'}, dimensions={0} | all-to-all | bytes 1048576 | tf_op jit(solution)/shard_map/all_to_all | solution.py:28
  147.3 0.1 convert_reduce_fusion
  147.4 0.1 multiply_reduce_fusion
  147.5 0.1 divide_convert_fusion
  147.6 0.3 broadcast_in_dim.8
  147.9 30.4 %all_to_all.53 = bf16[16,64,1024]{2,1,0:T(8,128)(2,1)S(1)} all-to-all(bf16[16,64,1024]{2,1,0:T(8,128)(2,1)S(1)} %broadcast_in_dim.8), channel_id=1, replica_groups=mesh['ylo'=2,'zhi'=4,'zlo'=2,'x'=4,'yhi'=4,'core'=2] {'ylo','zlo','x'}, dimensions={0} | all-to-all | bytes 4194304 | tf_op jit(solution)/shard_map/all_to_all | solution.py:28
  178.2 1.5 copy.5
  (2 shorter events, 0.0 us)

commit v8 on v6

--- a/solution.py
+++ b/solution.py
@@ -118,7 +118,7 @@
 
 
 def col_body(scale, kernel_ref, parts_ref, out_ref):
-    row_scale = 1.0 / (scale * jnp.sum(parts_ref[...], axis=0))
+    row_scale = 1.0 / (scale * jnp.sum(parts_ref[...].astype(jnp.float32), axis=0))
     totals = [None] * (kernel_ref.shape[1] // LANES)
     for r, rows in enumerate(blocks_of(kernel_ref.shape[0])):
         turned = down_rows(row_scale[r : r + 1, :])
@@ -192,7 +192,9 @@
         row_sums, *col_scale = on_chip(
             functools.partial(row_body, proto_count),
             (
-                jax.ShapeDtypeStruct((count(PROTOS), *line_rows), jnp.float32),
+                jax.ShapeDtypeStruct(
+                    (count(PROTOS), *line_rows), jnp.float32 if last else jnp.bfloat16
+                ),
                 *[jax.ShapeDtypeStruct(line_protos, jnp.float32)] * last,
             ),
             (kernel, col_parts),

time: 182 us -> 181 us (level)
  no operation moved by 1% of the time
where the time goes in v8:
time: 181 us; the launch traced here: 178 us
  blocking collectives  164 us (91%)
  Pallas kernels  6.4 us (4%)
  matrix products  4.95 us (3%)
    all_to_all x9, blocking collectives, exchange(): return lax.all_to_all(blocks, axes, 0, 0, tiled=True)  164 us

profile of v8, /device:TPU:56, one launch (start us, length us, event | category | flops | bytes accessed | tf_op | source)
XLA Modules:
  0.0 178.3 jit_solution(18284123416767676333)
XLA Ops:
  0.6 2.5 %shard_map.41 = (bf16[1024,1024]{1,0:T(8,128)(2,1)S(1)}, bf16[1024,1024]{1,0:T(8,128)(2,1)S(1)}, f32[8,128]{1,0:T(8,128)S(1)}, f32[8,128]{1,0:T(8,128)S(1)}) custom-call(bf16[1024,1024]{1,0:T(8,128)(2,1)} %rows_in.1, bf16[1024,1024]{1,0:T(8,128)(2,1)} %protos_in.1), custom_call_target="tpu_custom_call" | custom-call | flops 4194304 | bytes 8388608 | tf_op jit(solution)/shard_map/pallas_call | solution.py:85
  3.1 2.5 %fusion.2 = (bf16[1024]{0:T(1024)(128)(2,1)S(1)}, f32[1024,1024]{1,0:T(8,128)S(1)}) fusion(bf16[1024,1024]{1,0:T(8,128)(2,1)S(1)} %get-tuple-element.14, f32[1024]{0:T(1024)S(1)} %bitcast.10, bf16[1024,1024]{1,0:T(8,128)(2,1)S(1)} %get-tuple-element.12, f32[1024]{0:T(1024)S(1)} %bitcast.9), kind=kOutput, calls=%fused_computation.11 | convolution fusion | flops 2155871232 | bytes 8398848 | tf_op jit(solution)/shard_map/dot_general | solution.py:179
  5.7 24.7 %all_to_all.45.parts_ref = bf16[64,8,128]{2,1,0:T(8,128)(2,1)S(1)} all-to-all(bf16[64,8,128]{2,1,0:T(8,128)(2,1)S(1)} %broadcast_in_dim.6), channel_id=1, replica_groups=mesh['ylo'=2,'zhi'=4,'zlo'=2,'x'=4,'yhi'=4,'core'=2] {'ylo','zhi','zlo',..., dimensions={0} | all-to-all | bytes 262144 | tf_op jit(solution)/shard_map/all_to_all | solution.py:27
  30.4 0.4 shard_map.42
  30.8 11.0 %all_to_all.46.parts_ref = bf16[8,8,128]{2,1,0:T(8,128)(2,1)S(1)} all-to-all(bf16[8,8,128]{2,1,0:T(8,128)(2,1)S(1)} %shard_map.42), channel_id=1, replica_groups=mesh['ylo'=2,'zhi'=4,'zlo'=2,'x'=4,'yhi'=4,'core'=2] {'yhi','core'}, dimensions={0} | all-to-all | bytes 32768 | tf_op jit(solution)/shard_map/all_to_all | solution.py:27
  41.7 0.4 shard_map.43
  42.1 14.9 %all_to_all.47.parts_ref = bf16[64,8,128]{2,1,0:T(8,128)(2,1)S(1)} all-to-all(bf16[64,8,128]{2,1,0:T(8,128)(2,1)S(1)} %shard_map.43), channel_id=1, replica_groups=mesh['ylo'=2,'zhi'=4,'zlo'=2,'x'=4,'yhi'=4,'core'=2] {'ylo','zhi','zlo',..., dimensions={0} | all-to-all | bytes 262144 | tf_op jit(solution)/shard_map/all_to_all | solution.py:27
  57.0 0.4 shard_map.44
  57.5 10.1 %all_to_all.48.parts_ref = bf16[8,8,128]{2,1,0:T(8,128)(2,1)S(1)} all-to-all(bf16[8,8,128]{2,1,0:T(8,128)(2,1)S(1)} %shard_map.44), channel_id=1, replica_groups=mesh['ylo'=2,'zhi'=4,'zlo'=2,'x'=4,'yhi'=4,'core'=2] {'yhi','core'}, dimensions={0} | all-to-all | bytes 32768 | tf_op jit(solution)/shard_map/all_to_all | solution.py:27
  67.6 0.4 shard_map.45
  68.0 14.9 %all_to_all.49.parts_ref = bf16[64,8,128]{2,1,0:T(8,128)(2,1)S(1)} all-to-all(bf16[64,8,128]{2,1,0:T(8,128)(2,1)S(1)} %shard_map.45), channel_id=1, replica_groups=mesh['ylo'=2,'zhi'=4,'zlo'=2,'x'=4,'yhi'=4,'core'=2] {'ylo','zhi','zlo',..., dimensions={0} | all-to-all | bytes 262144 | tf_op jit(solution)/shard_map/all_to_all | solution.py:27
  82.9 0.4 shard_map.46
  83.3 10.2 %all_to_all.50.parts_ref = f32[8,8,128]{2,1,0:T(8,128)S(1)} all-to-all(f32[8,8,128]{2,1,0:T(8,128)S(1)} %get-tuple-element.16), channel_id=1, replica_groups=mesh['ylo'=2,'zhi'=4,'zlo'=2,'x'=4,'yhi'=4,'core'=2] {'yhi','core'}, dimensions={0} | all-to-all | bytes 65536 | tf_op jit(solution)/shard_map/all_to_all | solution.py:27
  93.5 0.6 shard_map.47.source
  94.1 2.4 %convolution_convert_fusion = bf16[1024,1024]{1,0:T(8,128)(2,1)S(1)} fusion(bf16[1024,1024]{1,0:T(8,128)(2,1)S(1)} %shard_map.47.source, bf16[1024,1024]{1,0:T(8,128)(2,1)S(1)} %get-tuple-element.12), kind=kOutput, calls=%fused_computation.5 | convolution fusion | flops 2148532224 | bytes 6291456 | tf_op jit(solution)/shard_map/dot_general | solution.py:223
  96.5 1.3 shard_map.48
  97.9 30.4 %all_to_all.51 = bf16[16,64,1024]{2,1,0:T(8,128)(2,1)S(1)} all-to-all(bf16[16,64,1024]{2,1,0:T(8,128)(2,1)S(1)} %bitcast.12), channel_id=1, replica_groups=mesh['ylo'=2,'zhi'=4,'zlo'=2,'x'=4,'yhi'=4,'core'=2] {'x','zlo','ylo'}, dimensions={0} | all-to-all | bytes 4194304 | tf_op jit(solution)/shard_map/all_to_all | solution.py:27
  128.3 0.4 reduce_sum.40
  128.7 0.1 broadcast_in_dim.7
  128.8 18.2 %all_to_all.52 = bf16[4,64,1024]{2,1,0:T(8,128)(2,1)S(1)} all-to-all(bf16[4,64,1024]{2,1,0:T(8,128)(2,1)S(1)} %broadcast_in_dim.7), channel_id=1, replica_groups=mesh['ylo'=2,'zhi'=4,'zlo'=2,'x'=4,'yhi'=4,'core'=2] {'zhi'}, dimensions={0} | all-to-all | bytes 1048576 | tf_op jit(solution)/shard_map/all_to_all | solution.py:27
  147.0 0.1 convert_reduce_fusion
  147.1 0.1 multiply_reduce_fusion
  147.2 0.1 divide_convert_fusion
  147.3 0.3 broadcast_in_dim.8
  147.6 29.4 %all_to_all.53 = bf16[16,64,1024]{2,1,0:T(8,128)(2,1)S(1)} all-to-all(bf16[16,64,1024]{2,1,0:T(8,128)(2,1)S(1)} %broadcast_in_dim.8), channel_id=1, replica_groups=mesh['ylo'=2,'zhi'=4,'zlo'=2,'x'=4,'yhi'=4,'core'=2] {'x','zlo','ylo'}, dimensions={0} | all-to-all | bytes 4194304 | tf_op jit(solution)/shard_map/all_to_all | solution.py:27
  177.0 1.3 copy.5
  (2 shorter events, 0.0 us)

commit v9 on v8

--- a/solution.py
+++ b/solution.py
@@ -134,41 +134,42 @@
     return (values.astype(jnp.float32) * inverse.reshape(-1, 1)).astype(jnp.bfloat16)
 
 
-def codes_body(scale, mass, kernel_ref, parts_ref, col_ref, codes_ref):
+def codes_body(scale, mass, parts, kernel_ref, parts_ref, col_ref, codes_ref, out_ref, sems):
     row_scale = mass / (scale * jnp.sum(parts_ref[...], axis=0))
     col_scale = col_ref[...]
+    size = kernel_ref.shape[0] // parts
+    copies = []
     for r, rows in enumerate(blocks_of(kernel_ref.shape[0])):
         turned = down_rows(row_scale[r : r + 1, :])
         for k, lanes in enumerate(blocks_of(kernel_ref.shape[1])):
             tile = turned * kernel_ref[rows, lanes] * col_scale[k : k + 1, :]
             codes_ref[rows, lanes] = tile.astype(jnp.bfloat16)
-
-
-def write_body(parts, source, target, sems):
-    size = source.shape[0] // parts
-    copies = []
-    for part in range(parts):
-        rows = pl.ds(part * size, size)
-        copy = pltpu.make_async_copy(source.at[rows, :], target.at[rows, :], sems.at[part])
-        copy.start()
-        copies.append(copy)
+        if rows.stop % size == 0:
+            done = pl.ds(rows.stop - size, size)
+            copy = pltpu.make_async_copy(
+                codes_ref.at[done, :], out_ref.at[done, :], sems.at[len(copies)]
+            )
+            copy.start()
+            copies.append(copy)
     for copy in copies:
         copy.wait()
 
 
-def write_out(array):
+def make_codes(scale, mass, kernel, row_parts, col_scale):
     parts = 4
+    vmem = pl.BlockSpec(memory_space=pltpu.VMEM)
+    shape = jax.ShapeDtypeStruct(kernel.shape, jnp.bfloat16)
     return pl.pallas_call(
-        functools.partial(write_body, parts),
-        out_shape=jax.ShapeDtypeStruct(array.shape, array.dtype),
-        in_specs=[pl.BlockSpec(memory_space=pltpu.VMEM)],
-        out_specs=pl.BlockSpec(memory_space=pl.ANY),
+        functools.partial(codes_body, scale, mass, parts),
+        out_shape=(shape, shape),
+        in_specs=[vmem] * 3,
+        out_specs=(vmem, pl.BlockSpec(memory_space=pl.ANY)),
         scratch_shapes=[pltpu.SemaphoreType.DMA((parts,))],
-        compiler_params=pltpu.CompilerParams(vmem_limit_bytes=8 * 1024 * 1024),
+        compiler_params=pltpu.CompilerParams(vmem_limit_bytes=40 * 1024 * 1024),
         cost_estimate=pl.CostEstimate(
-            flops=0, bytes_accessed=4 * array.size, transcendentals=0
+            flops=2 * kernel.size, bytes_accessed=8 * kernel.size, transcendentals=0
         ),
-    )(array)
+    )(kernel, row_parts, col_scale)
 
 
 def body(embeddings, prototypes):
@@ -212,19 +213,11 @@
             )
             col_parts = exchange(col_sums, ROWS)
     mass = row_count * proto_count
-    early_codes = on_chip(
-        functools.partial(codes_body, row_count, mass),
-        jax.ShapeDtypeStruct(kernel.shape, jnp.bfloat16),
-        (kernel, row_parts, col_scale[0]),
-        work,
-        3 * work,
-    )
+    early_codes, codes = make_codes(row_count, mass, kernel, row_parts, col_scale[0])
     feature_width = embeddings.shape[1]
     term = lax.dot_general(
         early_codes, embeddings, (((0,), (0,)), ((), ())), preferred_element_type=jnp.float32
     ).astype(jnp.bfloat16)
-    term, early_codes = lax.optimization_barrier((term, early_codes))
-    term, codes = lax.optimization_barrier((term, write_out(early_codes)))
     near = exchange(term.reshape(count(NEAR), -1, feature_width), NEAR)
     near = jnp.sum(near.astype(jnp.float32), axis=0).astype(jnp.bfloat16)
     sums = jnp.sum(everyone(near, FAR).astype(jnp.float32), axis=0)

time: 181 us -> 181 us (level)
  no operation moved by 1% of the time
where the time goes in v9:
time: 181 us; the launch traced here: 178 us
  blocking collectives  164 us (91%)
  Pallas kernels  6.04 us (3%)
  matrix products  4.95 us (3%)
    all_to_all x9, blocking collectives, exchange(): return lax.all_to_all(blocks, axes, 0, 0, tiled=True)  164 us

profile of v9, /device:TPU:56, one launch (start us, length us, event | category | flops | bytes accessed | tf_op | source)
XLA Modules:
  0.0 178.0 jit_solution(4417007412873726069)
XLA Ops:
  0.6 2.5 %shard_map.41 = (bf16[1024,1024]{1,0:T(8,128)(2,1)S(1)}, bf16[1024,1024]{1,0:T(8,128)(2,1)S(1)}, f32[8,128]{1,0:T(8,128)S(1)}, f32[8,128]{1,0:T(8,128)S(1)}) custom-call(bf16[1024,1024]{1,0:T(8,128)(2,1)} %rows_in.1, bf16[1024,1024]{1,0:T(8,128)(2,1)} %protos_in.1), custom_call_target="tpu_custom_call" | custom-call | flops 4194304 | bytes 8388608 | tf_op jit(solution)/shard_map/pallas_call | solution.py:85
  3.1 2.5 %fusion.2 = (bf16[1024]{0:T(1024)(128)(2,1)S(1)}, f32[1024,1024]{1,0:T(8,128)S(1)}) fusion(bf16[1024,1024]{1,0:T(8,128)(2,1)S(1)} %get-tuple-element.12, f32[1024]{0:T(1024)S(1)} %bitcast.10, bf16[1024,1024]{1,0:T(8,128)(2,1)S(1)} %get-tuple-element.10, f32[1024]{0:T(1024)S(1)} %bitcast.9), kind=kOutput, calls=%fused_computation.11 | convolution fusion | flops 2155871232 | bytes 8398848 | tf_op jit(solution)/shard_map/dot_general | solution.py:180
  5.7 24.7 %all_to_all.45.parts_ref = bf16[64,8,128]{2,1,0:T(8,128)(2,1)S(1)} all-to-all(bf16[64,8,128]{2,1,0:T(8,128)(2,1)S(1)} %broadcast_in_dim.6), channel_id=1, replica_groups=mesh['ylo'=2,'zhi'=4,'zlo'=2,'x'=4,'yhi'=4,'core'=2] {'ylo','zhi','zlo',..., dimensions={0} | all-to-all | bytes 262144 | tf_op jit(solution)/shard_map/all_to_all | solution.py:27
  30.4 0.4 shard_map.42
  30.8 11.0 %all_to_all.46.parts_ref = bf16[8,8,128]{2,1,0:T(8,128)(2,1)S(1)} all-to-all(bf16[8,8,128]{2,1,0:T(8,128)(2,1)S(1)} %shard_map.42), channel_id=1, replica_groups=mesh['ylo'=2,'zhi'=4,'zlo'=2,'x'=4,'yhi'=4,'core'=2] {'yhi','core'}, dimensions={0} | all-to-all | bytes 32768 | tf_op jit(solution)/shard_map/all_to_all | solution.py:27
  41.7 0.4 shard_map.43
  42.1 14.9 %all_to_all.47.parts_ref = bf16[64,8,128]{2,1,0:T(8,128)(2,1)S(1)} all-to-all(bf16[64,8,128]{2,1,0:T(8,128)(2,1)S(1)} %shard_map.43), channel_id=1, replica_groups=mesh['ylo'=2,'zhi'=4,'zlo'=2,'x'=4,'yhi'=4,'core'=2] {'ylo','zhi','zlo',..., dimensions={0} | all-to-all | bytes 262144 | tf_op jit(solution)/shard_map/all_to_all | solution.py:27
  57.0 0.4 shard_map.44
  57.5 10.1 %all_to_all.48.parts_ref = bf16[8,8,128]{2,1,0:T(8,128)(2,1)S(1)} all-to-all(bf16[8,8,128]{2,1,0:T(8,128)(2,1)S(1)} %shard_map.44), channel_id=1, replica_groups=mesh['ylo'=2,'zhi'=4,'zlo'=2,'x'=4,'yhi'=4,'core'=2] {'yhi','core'}, dimensions={0} | all-to-all | bytes 32768 | tf_op jit(solution)/shard_map/all_to_all | solution.py:27
  67.6 0.4 shard_map.45
  68.0 14.9 %all_to_all.49.parts_ref = bf16[64,8,128]{2,1,0:T(8,128)(2,1)S(1)} all-to-all(bf16[64,8,128]{2,1,0:T(8,128)(2,1)S(1)} %shard_map.45), channel_id=1, replica_groups=mesh['ylo'=2,'zhi'=4,'zlo'=2,'x'=4,'yhi'=4,'core'=2] {'ylo','zhi','zlo',..., dimensions={0} | all-to-all | bytes 262144 | tf_op jit(solution)/shard_map/all_to_all | solution.py:27
  82.9 0.4 shard_map.46
  83.3 10.2 %all_to_all.50.parts_ref = f32[8,8,128]{2,1,0:T(8,128)S(1)} all-to-all(f32[8,8,128]{2,1,0:T(8,128)S(1)} %get-tuple-element.14), channel_id=1, replica_groups=mesh['ylo'=2,'zhi'=4,'zlo'=2,'x'=4,'yhi'=4,'core'=2] {'yhi','core'}, dimensions={0} | all-to-all | bytes 65536 | tf_op jit(solution)/shard_map/all_to_all | solution.py:27
  93.5 1.5 shard_map.47
  95.1 2.4 %convolution_convert_fusion = bf16[1024,1024]{1,0:T(8,128)(2,1)S(1)} fusion(bf16[1024,1024]{1,0:T(8,128)(2,1)S(1)} %get-tuple-element.17, bf16[1024,1024]{1,0:T(8,128)(2,1)S(1)} %get-tuple-element.10), kind=kOutput, calls=%fused_computation.5 | convolution fusion | flops 2148532224 | bytes 6291456 | tf_op jit(solution)/shard_map/dot_general | solution.py:218
  97.5 30.4 %all_to_all.51 = bf16[16,64,1024]{2,1,0:T(8,128)(2,1)S(1)} all-to-all(bf16[16,64,1024]{2,1,0:T(8,128)(2,1)S(1)} %bitcast.12), channel_id=1, replica_groups=mesh['ylo'=2,'zhi'=4,'zlo'=2,'x'=4,'yhi'=4,'core'=2] {'x','zlo','ylo'}, dimensions={0} | all-to-all | bytes 4194304 | tf_op jit(solution)/shard_map/all_to_all | solution.py:27
  127.9 0.4 reduce_sum.40
  128.3 0.1 broadcast_in_dim.7
  128.4 18.2 %all_to_all.52 = bf16[4,64,1024]{2,1,0:T(8,128)(2,1)S(1)} all-to-all(bf16[4,64,1024]{2,1,0:T(8,128)(2,1)S(1)} %broadcast_in_dim.7), channel_id=1, replica_groups=mesh['ylo'=2,'zhi'=4,'zlo'=2,'x'=4,'yhi'=4,'core'=2] {'zhi'}, dimensions={0} | all-to-all | bytes 1048576 | tf_op jit(solution)/shard_map/all_to_all | solution.py:27
  146.6 0.1 convert_reduce_fusion
  146.7 0.1 multiply_reduce_fusion
  146.8 0.1 divide_convert_fusion
  147.0 0.3 broadcast_in_dim.8
  147.2 29.4 %all_to_all.53 = bf16[16,64,1024]{2,1,0:T(8,128)(2,1)S(1)} all-to-all(bf16[16,64,1024]{2,1,0:T(8,128)(2,1)S(1)} %broadcast_in_dim.8), channel_id=1, replica_groups=mesh['ylo'=2,'zhi'=4,'zlo'=2,'x'=4,'yhi'=4,'core'=2] {'x','zlo','ylo'}, dimensions={0} | all-to-all | bytes 4194304 | tf_op jit(solution)/shard_map/all_to_all | solution.py:27
  176.7 1.3 copy.5
  (2 shorter events, 0.0 us)

commit v10 on v9

--- a/solution.py
+++ b/solution.py
@@ -170,6 +170,17 @@
             flops=2 * kernel.size, bytes_accessed=8 * kernel.size, transcendentals=0
         ),
     )(kernel, row_parts, col_scale)
+
+
+def center_body(parts_ref, out_ref):
+    group = 16
+    width = parts_ref.shape[2]
+    for start in range(0, parts_ref.shape[1], group):
+        rows = slice(start, start + group)
+        sums = jnp.sum(parts_ref[:, rows, :].astype(jnp.float32), axis=0)
+        squares = jnp.sum(sums * sums, axis=1, keepdims=True)
+        scaled = (sums * (1.0 / jnp.sqrt(squares / width + 1e-06))).astype(jnp.bfloat16)
+        out_ref[:, rows, :] = jnp.broadcast_to(scaled[None], (out_ref.shape[0], group, width))
 
 
 def body(embeddings, prototypes):
@@ -220,10 +231,15 @@
     ).astype(jnp.bfloat16)
     near = exchange(term.reshape(count(NEAR), -1, feature_width), NEAR)
     near = jnp.sum(near.astype(jnp.float32), axis=0).astype(jnp.bfloat16)
-    sums = jnp.sum(everyone(near, FAR).astype(jnp.float32), axis=0)
-    squares = jnp.sum(sums * sums, axis=1, keepdims=True)
-    scaled = (sums / jnp.sqrt(squares / feature_width + 1e-06)).astype(jnp.bfloat16)
-    return (codes, everyone(scaled, NEAR).reshape(protos, feature_width))
+    far = everyone(near, FAR)
+    scaled = on_chip(
+        center_body,
+        jax.ShapeDtypeStruct((count(NEAR), *near.shape), jnp.bfloat16),
+        (far,),
+        8 * near.size,
+        40 * near.size,
+    )
+    return (codes, exchange(scaled, NEAR).reshape(protos, feature_width))
 
 
 def solution(mesh):

time: 181 us -> 181 us (level)
  no operation moved by 1% of the time
where the time goes in v10:
time: 181 us; the launch traced here: 178 us
  blocking collectives  164 us (91%)
  Pallas kernels  6.28 us (3%)
  matrix products  4.95 us (3%)
    all_to_all x9, blocking collectives, exchange(): return lax.all_to_all(blocks, axes, 0, 0, tiled=True)  164 us

profile of v10, /device:TPU:56, one launch (start us, length us, event | category | flops | bytes accessed | tf_op | source)
XLA Modules:
  0.0 177.6 jit_solution(10306969412021948008)
XLA Ops:
  0.6 2.5 %shard_map.41 = (bf16[1024,1024]{1,0:T(8,128)(2,1)S(1)}, bf16[1024,1024]{1,0:T(8,128)(2,1)S(1)}, f32[8,128]{1,0:T(8,128)S(1)}, f32[8,128]{1,0:T(8,128)S(1)}) custom-call(bf16[1024,1024]{1,0:T(8,128)(2,1)} %rows_in.1, bf16[1024,1024]{1,0:T(8,128)(2,1)} %protos_in.1), custom_call_target="tpu_custom_call" | custom-call | flops 4194304 | bytes 8388608 | tf_op jit(solution)/shard_map/pallas_call | solution.py:85
  3.1 2.5 %fusion.2 = (bf16[1024]{0:T(1024)(128)(2,1)S(1)}, f32[1024,1024]{1,0:T(8,128)S(1)}) fusion(bf16[1024,1024]{1,0:T(8,128)(2,1)S(1)} %get-tuple-element.12, f32[1024]{0:T(1024)S(1)} %bitcast.10, bf16[1024,1024]{1,0:T(8,128)(2,1)S(1)} %get-tuple-element.10, f32[1024]{0:T(1024)S(1)} %bitcast.9), kind=kOutput, calls=%fused_computation.7 | convolution fusion | flops 2155871232 | bytes 8398848 | tf_op jit(solution)/shard_map/dot_general | solution.py:191
  5.7 24.7 %all_to_all.45.parts_ref = bf16[64,8,128]{2,1,0:T(8,128)(2,1)S(1)} all-to-all(bf16[64,8,128]{2,1,0:T(8,128)(2,1)S(1)} %broadcast_in_dim.4), channel_id=1, replica_groups=mesh['ylo'=2,'zhi'=4,'zlo'=2,'x'=4,'yhi'=4,'core'=2] {'ylo','zhi','zlo',..., dimensions={0} | all-to-all | bytes 262144 | tf_op jit(solution)/shard_map/all_to_all | solution.py:27
  30.4 0.4 shard_map.42
  30.8 11.0 %all_to_all.46.parts_ref = bf16[8,8,128]{2,1,0:T(8,128)(2,1)S(1)} all-to-all(bf16[8,8,128]{2,1,0:T(8,128)(2,1)S(1)} %shard_map.42), channel_id=1, replica_groups=mesh['ylo'=2,'zhi'=4,'zlo'=2,'x'=4,'yhi'=4,'core'=2] {'yhi','core'}, dimensions={0} | all-to-all | bytes 32768 | tf_op jit(solution)/shard_map/all_to_all | solution.py:27
  41.7 0.4 shard_map.43
  42.1 14.9 %all_to_all.47.parts_ref = bf16[64,8,128]{2,1,0:T(8,128)(2,1)S(1)} all-to-all(bf16[64,8,128]{2,1,0:T(8,128)(2,1)S(1)} %shard_map.43), channel_id=1, replica_groups=mesh['ylo'=2,'zhi'=4,'zlo'=2,'x'=4,'yhi'=4,'core'=2] {'ylo','zhi','zlo',..., dimensions={0} | all-to-all | bytes 262144 | tf_op jit(solution)/shard_map/all_to_all | solution.py:27
  57.0 0.4 shard_map.44
  57.5 10.1 %all_to_all.48.parts_ref = bf16[8,8,128]{2,1,0:T(8,128)(2,1)S(1)} all-to-all(bf16[8,8,128]{2,1,0:T(8,128)(2,1)S(1)} %shard_map.44), channel_id=1, replica_groups=mesh['ylo'=2,'zhi'=4,'zlo'=2,'x'=4,'yhi'=4,'core'=2] {'yhi','core'}, dimensions={0} | all-to-all | bytes 32768 | tf_op jit(solution)/shard_map/all_to_all | solution.py:27
  67.6 0.4 shard_map.45
  68.0 14.9 %all_to_all.49.parts_ref = bf16[64,8,128]{2,1,0:T(8,128)(2,1)S(1)} all-to-all(bf16[64,8,128]{2,1,0:T(8,128)(2,1)S(1)} %shard_map.45), channel_id=1, replica_groups=mesh['ylo'=2,'zhi'=4,'zlo'=2,'x'=4,'yhi'=4,'core'=2] {'ylo','zhi','zlo',..., dimensions={0} | all-to-all | bytes 262144 | tf_op jit(solution)/shard_map/all_to_all | solution.py:27
  82.9 0.4 shard_map.46
  83.3 10.2 %all_to_all.50.parts_ref = f32[8,8,128]{2,1,0:T(8,128)S(1)} all-to-all(f32[8,8,128]{2,1,0:T(8,128)S(1)} %get-tuple-element.14), channel_id=1, replica_groups=mesh['ylo'=2,'zhi'=4,'zlo'=2,'x'=4,'yhi'=4,'core'=2] {'yhi','core'}, dimensions={0} | all-to-all | bytes 65536 | tf_op jit(solution)/shard_map/all_to_all | solution.py:27
  93.5 1.5 shard_map.47
  95.1 2.4 %convolution_convert_fusion = bf16[1024,1024]{1,0:T(8,128)(2,1)S(1)} fusion(bf16[1024,1024]{1,0:T(8,128)(2,1)S(1)} %get-tuple-element.17, bf16[1024,1024]{1,0:T(8,128)(2,1)S(1)} %get-tuple-element.10), kind=kOutput, calls=%fused_computation.5 | convolution fusion | flops 2148532224 | bytes 6291456 | tf_op jit(solution)/shard_map/dot_general | solution.py:229
  97.5 30.4 %all_to_all.51 = bf16[16,64,1024]{2,1,0:T(8,128)(2,1)S(1)} all-to-all(bf16[16,64,1024]{2,1,0:T(8,128)(2,1)S(1)} %bitcast.12), channel_id=1, replica_groups=mesh['ylo'=2,'zhi'=4,'zlo'=2,'x'=4,'yhi'=4,'core'=2] {'x','zlo','ylo'}, dimensions={0} | all-to-all | bytes 4194304 | tf_op jit(solution)/shard_map/all_to_all | solution.py:27
  127.9 0.4 reduce_sum.22
  128.3 0.1 broadcast_in_dim.5
  128.4 18.2 %all_to_all.52.parts_ref = bf16[4,64,1024]{2,1,0:T(8,128)(2,1)S(1)} all-to-all(bf16[4,64,1024]{2,1,0:T(8,128)(2,1)S(1)} %broadcast_in_dim.5), channel_id=1, replica_groups=mesh['ylo'=2,'zhi'=4,'zlo'=2,'x'=4,'yhi'=4,'core'=2] {'zhi'}, dimensions={0} | all-to-all | bytes 1048576 | tf_op jit(solution)/shard_map/all_to_all | solution.py:27
  146.6 0.2 shard_map.48
  146.9 29.4 %all_to_all.53 = bf16[16,64,1024]{2,1,0:T(8,128)(2,1)S(1)} all-to-all(bf16[16,64,1024]{2,1,0:T(8,128)(2,1)S(1)} %shard_map.48), channel_id=1, replica_groups=mesh['ylo'=2,'zhi'=4,'zlo'=2,'x'=4,'yhi'=4,'core'=2] {'x','zlo','ylo'}, dimensions={0} | all-to-all | bytes 4194304 | tf_op jit(solution)/shard_map/all_to_all | solution.py:27
  176.3 1.3 copy.5
  (1 shorter events, 0.0 us)
